TPU v7x, 256 devices: a whole 4x4x8 slice. The times are simulated.
256 devices in a mesh: seq: 16 (over z, x_lo), expert: 8 (over y, core), ffn: 2 (over x_hi).
Axes of the slice: x: 4 (x_hi: 2, x_lo: 2; x = x_hi * 2 + x_lo), y: 4, z: 8, core: 2. Of those that a mesh axis runs over, the one named last changes fastest.
Arguments:
- queries: bfloat16 [2048, 4096], P('seq', ('expert', 'ffn')), may hold values from -122 to 122
- keys: bfloat16 [2048, 1024], P('seq', 'expert'), may hold values from -4.1 to 4.1
- values: bfloat16 [2048, 1024], P('seq', 'expert'), may hold values from -6 to 6
- residual_in: bfloat16 [2048, 4096], P('seq', ('expert', 'ffn')), may hold values from -6 to 6
- routes: int32 [2048, 2], P('seq'), may hold values from 0 to 7, all different within a row; in each aligned block of 128 rows (0 to 127, 128 to 255, ...) at most 48 rows name the same one
- router: bfloat16 [4096, 8], replicated, may hold values from -0.09375 to 0.09375
- w_gate: bfloat16 [8, 4096, 14336], P('expert', None, ('seq', 'ffn')), may hold values from -0.09375 to 0.09375
- w_up: bfloat16 [8, 4096, 14336], P('expert', None, ('seq', 'ffn')), may hold values from -0.09375 to 0.09375
- w_down: bfloat16 [8, 14336, 4096], P('expert', ('seq', 'ffn')), may hold values from -0.046875 to 0.046875
Outputs:
- block_out: bfloat16 [2048, 4096], P('seq', ('expert', 'ffn'))
Inputs may be any that keep to these rules, and one draw needn't show every extreme that they name: `routes`: each token names two different experts; among the 128 tokens of one index of seq no expert is named more than 48 times, a bound that some block reaches.
All inputs are finite; a program needn't handle non-finite values.
Results may differ from a plain program's by a relative error of at most 0.0052.
Values may be sent and summed in bfloat16 or wider, within the bound.
No kernel may reach another device: no remote copies, remote signals or barrier semaphores. Data moves between devices by JAX's collectives and lax.ppermute only.
A program may use at most 128 MiB of HBM per device.

v0:
```python
import functools

import jax
import jax.numpy as jnp
from jax import lax
from jax.experimental import pallas as pl
from jax.experimental.pallas import tpu as pltpu
from jax.sharding import PartitionSpec as P

HEADS = 32
KV_HEADS = 8
HEAD_DIM = 128
NZ, NX, NY = 8, 4, 4
ALL = ("seq", "expert", "ffn")


def place_of(z, x, y, core):
    return ((z * 2 + x % 2) * 2 * NY + y * 2 + core) * 2 + x // 2


def hop(value, core_0, core_1):
    pairs = []
    for core, by in enumerate((core_0, core_1)):
        if by is None:
            continue
        dz, dx = by
        for z in range(NZ):
            for x in range(NX):
                for y in range(NY):
                    to = place_of((z + dz) % NZ, (x + dx) % NX, y, core)
                    pairs.append((place_of(z, x, y, core), to))
    return lax.ppermute(value, ALL, pairs)


def expert_kernel(places, outs, tile, *refs):
    pieces = refs[: len(places)]
    gate_ref, up_ref, down_ref = refs[len(places) : len(places) + 3]
    out_refs = refs[len(places) + 3 : len(places) + 3 + len(outs)]
    rows_ref, gate_sum, up_sum, hidden = refs[len(places) + 3 + len(outs) :]
    step = pl.program_id(0)
    steps_in = rows_ref.shape[0]
    across = (((1,), (1,)), ((), ()))

    @pl.when(step == 0)
    def _():
        for (row, col), piece in zip(places, pieces):
            count, width = piece.shape
            for k in range(width // tile):
                rows_ref[col // tile + k, row : row + count, :] = piece[:, k * tile : (k + 1) * tile]
        gate_sum[...] = jnp.zeros_like(gate_sum)
        up_sum[...] = jnp.zeros_like(up_sum)

    @pl.when(step < steps_in)
    def _():
        rows = rows_ref[step]
        gate_sum[...] += lax.dot_general(
            rows, gate_ref[...], across, preferred_element_type=jnp.float32
        )
        up_sum[...] += lax.dot_general(
            rows, up_ref[...], across, preferred_element_type=jnp.float32
        )

    @pl.when(step == steps_in - 1)
    def _():
        value = gate_sum[...]
        hidden[...] = (value / (1.0 + jnp.exp(-value)) * up_sum[...]).astype(jnp.bfloat16)

    for k in range(steps_in):

        @pl.when(step == steps_in + k)
        def _():
            result = jnp.dot(hidden[...], down_ref[...], preferred_element_type=jnp.float32)
            for (row, count, begin, number), out in zip(outs, out_refs):
                if begin <= k < begin + number:
                    out[...] = result[row : row + count]


def expert(groups, gate_t, up_t, down_w, tile=1024):
    units, width = gate_t.shape
    steps = width // tile
    places, outs, arrays, shapes, row = [], [], [], [], 0
    for group in groups:
        col = 0
        for piece in group:
            places.append((row, col))
            outs.append((row, piece.shape[0], col // tile, piece.shape[1] // tile))
            shapes.append(jax.ShapeDtypeStruct(piece.shape, jnp.float32))
            arrays.append(piece)
            col += piece.shape[1]
        row += group[0].shape[0]
    whole = [pl.BlockSpec(p.shape, lambda i: (0, 0)) for p in arrays]
    first = pl.BlockSpec((units, tile), lambda i: (0, jnp.minimum(i, steps - 1)))
    second = pl.BlockSpec((units, tile), lambda i: (0, jnp.maximum(i - steps, 0)))

    def part(begin, number):
        return lambda i: (0, jnp.clip(i - steps - begin, 0, number - 1))

    found = pl.pallas_call(
        functools.partial(expert_kernel, tuple(places), tuple(outs), tile),
        grid=(2 * steps,),
        in_specs=whole + [first, first, second],
        out_specs=[pl.BlockSpec((count, tile), part(b, n)) for _, count, b, n in outs],
        out_shape=shapes,
        scratch_shapes=[
            pltpu.VMEM((steps, row, tile), jnp.bfloat16),
            pltpu.VMEM((row, units), jnp.float32),
            pltpu.VMEM((row, units), jnp.float32),
            pltpu.VMEM((row, units), jnp.bfloat16),
        ],
        compiler_params=pltpu.CompilerParams(vmem_limit_bytes=32 * 1024 * 1024),
        cost_estimate=pl.CostEstimate(
            flops=6 * row * units * width,
            bytes_accessed=6 * units * width + 6 * row * width,
            transcendentals=row * units,
        ),
    )(*arrays, gate_t, up_t, down_w)
    found, results = list(found), []
    for group in groups:
        results.append([found.pop(0) for _ in group])
    return results


def attention(queries, key_all, value_all, q_pos):
    tok = queries.shape[0]
    heads = queries.shape[1] // HEAD_DIM
    q_heads = queries.reshape(tok, heads, HEAD_DIM)
    scores = jnp.einsum("qhd,kd->hqk", q_heads, key_all, preferred_element_type=jnp.float32)
    scores = scores * HEAD_DIM ** (-0.5)
    allowed = jnp.arange(key_all.shape[0])[None, None, :] <= q_pos[None, :, None]
    masked = jnp.where(allowed, scores, -1e30)
    high = jnp.max(masked, axis=2, keepdims=True)
    probs = jnp.where(allowed, jnp.exp(masked - high), 0.0)
    total = jnp.sum(probs, axis=2, keepdims=True)
    accum = jnp.einsum(
        "hqk,kd->hqd", probs, value_all.astype(jnp.float32), precision=lax.Precision.HIGHEST
    )
    return (accum / total).transpose(1, 0, 2).reshape(tok, heads * HEAD_DIM)


def shards(queries, keys, values, residual_in, routes, router, w_gate, w_up, w_down):
    n_exp = lax.axis_size("expert")
    n_ffn = lax.axis_size("ffn")
    n_seq = lax.axis_size("seq")
    seq_pos = lax.axis_index("seq")
    exp_pos = lax.axis_index("expert")
    ffn_pos = lax.axis_index("ffn")
    tok = queries.shape[0]
    width = router.shape[0]
    span = residual_in.shape[1]
    capacity = 3 * tok // n_exp
    half_cap = capacity // n_ffn

    pair = jnp.concatenate([keys, values], axis=1)
    pairs = lax.all_to_all(
        jnp.broadcast_to(pair[None], (n_seq,) + pair.shape), "seq", 0, 0, tiled=True
    ).reshape(n_seq * tok, pair.shape[1])
    key_all, value_all = pairs[:, :HEAD_DIM], pairs[:, HEAD_DIM:]

    flat = routes.reshape(-1)
    partner_flat = routes[:, ::-1].reshape(-1)
    hot = (flat[:, None] == jnp.arange(n_exp)[None, :]).astype(jnp.int32)
    slot = jnp.sum((jnp.cumsum(hot, axis=0) - hot) * hot, axis=1)
    target = flat * capacity + slot
    placed = (jnp.arange(n_exp * capacity)[:, None] == target[None, :]).astype(jnp.int32)
    place_matrix = jnp.sum(placed.reshape(n_exp * capacity, tok, 2), axis=2).astype(jnp.bfloat16)

    q_pos = seq_pos * tok + jnp.arange(tok)
    attended = attention(queries, key_all, value_all, q_pos)
    mixed32 = residual_in.astype(jnp.float32) + attended
    mixed = mixed32.astype(jnp.bfloat16)

    buckets = jnp.dot(place_matrix, mixed, preferred_element_type=jnp.float32).astype(jnp.bfloat16)
    send = buckets.reshape(n_exp * n_ffn, half_cap, 1, span)
    rows = lax.all_to_all(
        send, ("expert", "ffn"), split_axis=0, concat_axis=2, tiled=True
    ).reshape(half_cap, width)

    partner_slots = jnp.sum(placed * partner_flat[None, :], axis=1).reshape(n_exp * n_ffn, half_cap)
    partner = lax.dynamic_slice_in_dim(partner_slots, exp_pos * n_ffn + ffn_pos, 1, 0)[0]
    logits = jnp.dot(rows, router, preferred_element_type=jnp.float32)
    ids = jnp.arange(n_exp)[None, :]
    own = jnp.sum(jnp.where(ids == exp_pos, logits, 0.0), axis=1)
    other = jnp.sum(jnp.where(ids == partner[:, None], logits, 0.0), axis=1)
    weight = 1.0 / (1.0 + jnp.exp(other - own))

    weights = (w_gate[0].T, w_up[0].T, w_down[0])
    zero_core = exp_pos % 2 == 0
    n = half_cap
    block = 4 * n

    def f32(v):
        return v.astype(jnp.float32)

    def b16(v):
        return v.astype(jnp.bfloat16)

    def pick(first, second):
        return jnp.where(zero_core, first, second)

    def pair(sums):
        return [v[0] for v in sums]

    near = [
        hop(rows, (0, -1), (-1, 0)),
        hop(rows, (0, 1), (1, 0)),
        hop(rows, (0, 2), (4, 0)),
    ]
    own = jnp.concatenate([rows] + near, axis=0)
    plus, minus = [None], [None]
    plus.append(hop(own, (-1, 0), (0, -1)))
    minus.append(hop(own, (1, 0), (0, 1)))
    next_plus = hop(own[: 2 * n], None, (-2, 0))
    next_minus = hop(jnp.concatenate([rows, near[1]], axis=0), None, (2, 0))
    other = jnp.concatenate([next_plus, next_minus], axis=0)
    ((sum_own,),) = expert([[own]], *weights)
    sum_own, minus[1] = lax.optimization_barrier((sum_own, minus[1]))
    plus.append(hop(pick(plus[1], other), (-1, 0), (0, -1)))
    minus.append(hop(pick(minus[1], other), (1, 0), (0, 1)))
    sums = {1: pair(expert([[plus[1]], [minus[1]]], *weights))}
    sums[1], minus[2] = lax.optimization_barrier((sums[1], minus[2]))
    plus.append(hop(pick(plus[2], plus[1]), (-1, 0), (0, -1)))
    minus.append(hop(minus[2], (1, 0), (0, 1)))
    sums[2] = pair(expert([[plus[2]], [minus[2]]], *weights))
    sums[2], minus[3] = lax.optimization_barrier((sums[2], minus[3]))
    far_plus = hop(plus[3][: 2 * n], (-1, 0), None)
    far_minus = hop(minus[3][2 * n :], (1, 0), None)
    sums[3] = pair(expert([[plus[3]], [minus[3]]], *weights))
    sums[3], far_minus = lax.optimization_barrier((sums[3], far_minus))
    last = pick(jnp.concatenate([far_plus, far_minus], axis=0), other)
    ((sum_last,),) = expert([[last]], *weights)

    turn_plus = hop(b16(sum_last[: 2 * n]), (1, 0), None)
    turn_minus = hop(b16(sum_last[2 * n :]), (-1, 0), None)
    go_plus = sums[3][0] + jnp.pad(f32(turn_plus), ((0, 2 * n), (0, 0)))
    go_minus = sums[3][1] + jnp.pad(f32(turn_minus), ((2 * n, 0), (0, 0)))
    plus_2, minus_2 = hop(b16(go_plus), (1, 0), (0, 1)), hop(b16(go_minus), (-1, 0), (0, -1))
    go_plus = pick(sums[2][0], sums[1][0]) + f32(plus_2)
    go_minus = sums[2][1] + f32(minus_2)
    plus_3, minus_3 = hop(b16(go_plus), (1, 0), (0, 1)), hop(b16(go_minus), (-1, 0), (0, -1))
    go_plus = pick(sums[1][0] + f32(plus_3), sums[2][0])
    go_minus = sums[1][1] + pick(f32(minus_3), 0.0)
    plus_4, minus_4 = hop(b16(go_plus), (1, 0), (0, 1)), hop(b16(go_minus), (-1, 0), (0, -1))
    total = sum_own + f32(pick(plus_4, plus_3)) + f32(minus_4)
    rest = b16(sum_last + f32(minus_3) + f32(plus_4))
    from_minus, from_plus = hop(rest[: 2 * n], None, (2, 0)), hop(rest[2 * n :], None, (-2, 0))
    chunk = [total[k * n : (k + 1) * n] for k in range(4)]
    chunk_1 = chunk[1] + f32(from_minus[n:])
    chunk_2 = chunk[2] + f32(from_plus[n:])
    result = chunk[0] + f32(from_minus[:n]) + f32(from_plus[:n])
    result = result + f32(hop(b16(chunk[3]), (0, 2), (4, 0)))
    result = result + f32(hop(b16(chunk_1), (0, 1), (1, 0)))
    result = result + f32(hop(b16(chunk_2), (0, -1), (-1, 0)))

    back = (result * weight[:, None]).astype(jnp.bfloat16).reshape(half_cap, n_exp * n_ffn, span)
    returned = lax.all_to_all(
        back, ("expert", "ffn"), split_axis=1, concat_axis=0, tiled=True
    ).reshape(n_exp * capacity, span)
    moe = jnp.einsum("st,sd->td", place_matrix, returned, preferred_element_type=jnp.float32)
    return (mixed32 + moe).astype(jnp.bfloat16)


def solution(mesh):
    placed = (
        P("seq", ("expert", "ffn")),
        P("seq", "expert"),
        P("seq", "expert"),
        P("seq", ("expert", "ffn")),
        P("seq", None),
        P(),
        P("expert", None, ("seq", "ffn")),
        P("expert", None, ("seq", "ffn")),
        P("expert", ("seq", "ffn"), None),
    )
    return jax.shard_map(
        shards, mesh=mesh, in_specs=placed, out_specs=P("seq", ("expert", "ffn")), check_vma=False
    )
```

profile of v0, /device:TPU:1, one launch (start us, length us, event | category | flops | bytes accessed | tf_op | source)
XLA Modules:
  0.0 234.2 jit_solution(817307322208640131)
XLA Ops:
  0.8 1.1 broadcast_in_dim.52
  1.9 10.0 %all-to-all-start = ((bf16[16,128,256]{2,1,0:T(8,128)(2,1)}), bf16[16,128,256]{2,1,0:T(8,128)(2,1)S(1)}, u32[]{:S(2)}, u32[]{:S(2)}) async-start(bf16[16,128,256]{2,1,0:T(8,128)(2,1)} %broadcast_in_dim.52), calls=%async_computation | async-start | bytes 2097152 | tf_op jit(solution)/shard_map/all_to_all | solution.py:154
  13.8 23.5 %all-to-all-done = bf16[16,128,256]{2,1,0:T(8,128)(2,1)S(1)} async-done(((bf16[16,128,256]{2,1,0:T(8,128)(2,1)}), bf16[16,128,256]{2,1,0:T(8,128)(2,1)S(1)}, u32[]{:S(2)}, u32[]{:S(2)}) %all-to-all-start) | async-done | bytes 1048608 | tf_op jit(solution)/shard_map/all_to_all | solution.py:154
  38.2 1.3 fusion.9
  39.7 0.9 convolution_convert_fusion
  40.5 11.0 %all-to-all-start.1 = ((bf16[16,24,1,256]{3,1,2,0:T(8,128)(2,1)}), bf16[16,24,1,256]{3,1,2,0:T(8,128)(2,1)S(1)}, u32[]{:S(2)}, u32[]{:S(2)}) async-start(bf16[16,24,1,256]{3,1,2,0:T(8,128)(2,1)} %bitcast.10), calls=%async_computation.1 | async-start | bytes 393216 | tf_op jit(solution)/shard_map/all_to_all | solution.py:174
  51.5 8.3 %all-to-all-done.1 = bf16[16,24,1,256]{3,1,2,0:T(8,128)(2,1)S(1)} async-done(((bf16[16,24,1,256]{3,1,2,0:T(8,128)(2,1)}), bf16[16,24,1,256]{3,1,2,0:T(8,128)(2,1)S(1)}, u32[]{:S(2)}, u32[]{:S(2)}) %all-to-all-start.1) | async-done | bytes 196640 | tf_op jit(solution)/shard_map/all_to_all | solution.py:174
  59.8 1.2 collective-permute-start.2
  61.4 2.3 collective-permute-start
  63.8 6.9 %collective-permute-done.1 = bf16[24,4096]{1,0:T(8,128)(2,1)S(1)} collective-permute-done((bf16[24,4096]{1,0:T(8,128)(2,1)S(1)}, bf16[24,4096]{1,0:T(8,128)(2,1)S(1)}, u32[]{:S(2)}, u32[]{:S(2)}) %collective-permute-start.1) | collective-permute-done | bytes 196640 | tf_op jit(solution)/shard_map/ppermute | solution.py:32
  70.7 3.4 %collective-permute-start.5 = (bf16[48,4096]{1,0:T(8,128)(2,1)S(1)}, bf16[48,4096]{1,0:T(8,128)(2,1)S(1)}, u32[]{:S(2)}, u32[]{:S(2)}) collective-permute-start(bf16[48,4096]{1,0:T(8,128)(2,1)S(1)} %get-tuple-element.52), channel_id=1, source_target_pairs={{2,194},{6,198},{10,202},{14,206},{18,210},{22,214},{26,218},{30,2... | collective-permute-start | bytes 1179656 | tf_op jit(solution)/shard_map/ppermute | solution.py:32
  74.2 1.5 collective-permute-start.3
  75.7 2.8 %collective-permute-start.6 = (bf16[48,4096]{1,0:T(8,128)(2,1)S(1)}, bf16[48,4096]{1,0:T(8,128)(2,1)S(1)}, u32[]{:S(2)}, u32[]{:S(2)}) collective-permute-start(bf16[48,4096]{1,0:T(8,128)(2,1)S(1)} %get-tuple-element.51), channel_id=1, source_target_pairs={{2,66},{6,70},{10,74},{14,78},{18,82},{22,86},{26,90},{30,94},{3,6... | collective-permute-start | bytes 1179656 | tf_op jit(solution)/shard_map/ppermute | solution.py:32
  78.5 2.0 copy-done.1
  80.6 2.0 copy-done.3
  82.6 2.0 copy-done.4
  84.6 5.3 %shard_map.91 = f32[96,4096]{1,0:T(8,128)S(1)} custom-call(bf16[96,4096]{1,0:T(8,128)(2,1)S(1)} %constant_dynamic-update-slice_fusion.refs_0_, bf16[448,4096]{1,0:T(8,128)(2,1)S(1)} %bitcast.69, bf16[448,4096]{1,0:T(8,128)(2,1)S(1)} %bitcast.74, bf16[448,4096]{1,0:T(8,128)(2,1)S(1)} %bitcast.79), custom_call_target="tpu_custom_call" | custom-call | flops 1056964608 | bytes 13369344 | tf_op jit(solution)/shard_map/pallas_call | solution.py:98
  90.0 1.4 collective-permute-done.6
  91.6 2.7 %collective-permute-start.8 = (bf16[96,4096]{1,0:T(8,128)(2,1)S(1)}, bf16[96,4096]{1,0:T(8,128)(2,1)S(1)}, u32[]{:S(2)}, u32[]{:S(2)}) collective-permute-start(bf16[96,4096]{1,0:T(8,128)(2,1)S(1)} %get-tuple-element.49), channel_id=1, source_target_pairs={{0,224},{4,228},{8,232},{12,236},{16,240},{20,244},{24,248},{28,25... | collective-permute-start | bytes 2359304 | tf_op jit(solution)/shard_map/ppermute | solution.py:32
  94.3 6.0 %shard_map.92 = (f32[96,4096]{1,0:T(8,128)S(1)}, f32[96,4096]{1,0:T(8,128)S(1)}) custom-call(bf16[96,4096]{1,0:T(8,128)(2,1)S(1)} %collective-permute-done.4.refs_0_, bf16[96,4096]{1,0:T(8,128)(2,1)S(1)} %collective-permute-done.3.refs_1_, bf16[448,4096]{1,0:T(8,128)(2,1)S(1)} %bitcast.70, bf16[448,4096]{1,0:T(8,128)(2,1)S(1)} %bitcast.75, ...), custom_call_target="tpu_custom_call" | custom-call | flops 2113929216 | bytes 15728640 | tf_op jit(solution)/shard_map/pallas_call | solution.py:98
  100.3 3.7 %collective-permute-done.7.refs_1_ = bf16[96,4096]{1,0:T(8,128)(2,1)S(1)} collective-permute-done((bf16[96,4096]{1,0:T(8,128)(2,1)S(1)}, bf16[96,4096]{1,0:T(8,128)(2,1)S(1)}, u32[]{:S(2)}, u32[]{:S(2)}) %collective-permute-start.7) | collective-permute-done | bytes 786464 | tf_op jit(solution)/shard_map/ppermute | solution.py:32
  104.0 2.8 %collective-permute-start.10 = (bf16[96,4096]{1,0:T(8,128)(2,1)S(1)}, bf16[96,4096]{1,0:T(8,128)(2,1)S(1)}, u32[]{:S(2)}, u32[]{:S(2)}) collective-permute-start(bf16[96,4096]{1,0:T(8,128)(2,1)S(1)} %broadcast_select_fusion), channel_id=1, source_target_pairs={{0,224},{4,228},{8,232},{12,236},{16,240},{20,244},{24,248},{28,25... | collective-permute-start | bytes 2359304 | tf_op jit(solution)/shard_map/ppermute | solution.py:32
  106.8 6.0 %shard_map.93 = (f32[96,4096]{1,0:T(8,128)S(1)}, f32[96,4096]{1,0:T(8,128)S(1)}) custom-call(bf16[96,4096]{1,0:T(8,128)(2,1)S(1)} %collective-permute-done.8.refs_0_, bf16[96,4096]{1,0:T(8,128)(2,1)S(1)} %collective-permute-done.7.refs_1_, bf16[448,4096]{1,0:T(8,128)(2,1)S(1)} %bitcast.71, bf16[448,4096]{1,0:T(8,128)(2,1)S(1)} %bitcast.76, ...), custom_call_target="tpu_custom_call" | custom-call | flops 2113929216 | bytes 15728640 | tf_op jit(solution)/shard_map/pallas_call | solution.py:98
  112.8 3.5 %collective-permute-done.9.refs_1_ = bf16[96,4096]{1,0:T(8,128)(2,1)S(1)} collective-permute-done((bf16[96,4096]{1,0:T(8,128)(2,1)S(1)}, bf16[96,4096]{1,0:T(8,128)(2,1)S(1)}, u32[]{:S(2)}, u32[]{:S(2)}) %collective-permute-start.9) | collective-permute-done | bytes 786464 | tf_op jit(solution)/shard_map/ppermute | solution.py:32
  117.8 6.0 %shard_map.94 = (f32[96,4096]{1,0:T(8,128)S(1)}, f32[96,4096]{1,0:T(8,128)S(1)}) custom-call(bf16[96,4096]{1,0:T(8,128)(2,1)S(1)} %collective-permute-done.10.refs_0_, bf16[96,4096]{1,0:T(8,128)(2,1)S(1)} %collective-permute-done.9.refs_1_, bf16[448,4096]{1,0:T(8,128)(2,1)S(1)} %bitcast.72, bf16[448,4096]{1,0:T(8,128)(2,1)S(1)} %bitcast.77, ...), custom_call_target="tpu_custom_call" | custom-call | flops 2113929216 | bytes 15728640 | tf_op jit(solution)/shard_map/pallas_call | solution.py:98
  124.0 5.3 %shard_map.95 = f32[96,4096]{1,0:T(8,128)S(1)} custom-call(bf16[96,4096]{1,0:T(8,128)(2,1)S(1)} %maximum_select_fusion.refs_0_, bf16[448,4096]{1,0:T(8,128)(2,1)S(1)} %bitcast.73, bf16[448,4096]{1,0:T(8,128)(2,1)S(1)} %bitcast.78, bf16[448,4096]{1,0:T(8,128)(2,1)S(1)} %bitcast.83), custom_call_target="tpu_custom_call" | custom-call | flops 1056964608 | bytes 13369344 | tf_op jit(solution)/shard_map/pallas_call | solution.py:98
  131.0 1.9 collective-permute-start.18
  133.1 9.1 %collective-permute-done.18 = bf16[96,4096]{1,0:T(8,128)(2,1)S(1)} collective-permute-done((bf16[96,4096]{1,0:T(8,128)(2,1)S(1)}, bf16[96,4096]{1,0:T(8,128)(2,1)S(1)}, u32[]{:S(2)}, u32[]{:S(2)}) %collective-permute-start.18) | collective-permute-done | bytes 786464 | tf_op jit(solution)/shard_map/ppermute | solution.py:32
  142.4 3.0 %collective-permute-start.19 = (bf16[96,4096]{1,0:T(8,128)(2,1)S(1)}, bf16[96,4096]{1,0:T(8,128)(2,1)S(1)}, u32[]{:S(2)}, u32[]{:S(2)}) collective-permute-start(bf16[96,4096]{1,0:T(8,128)(2,1)S(1)} %add_convert_fusion), channel_id=1, source_target_pairs={{0,224},{4,228},{8,232},{12,236},{16,240},{20,244},{24,248},{28,25... | collective-permute-start | bytes 2359304 | tf_op jit(solution)/shard_map/ppermute | solution.py:32
  145.8 8.6 %collective-permute-done.19 = bf16[96,4096]{1,0:T(8,128)(2,1)S(1)} collective-permute-done((bf16[96,4096]{1,0:T(8,128)(2,1)S(1)}, bf16[96,4096]{1,0:T(8,128)(2,1)S(1)}, u32[]{:S(2)}, u32[]{:S(2)}) %collective-permute-start.19) | collective-permute-done | bytes 786464 | tf_op jit(solution)/shard_map/ppermute | solution.py:32
  154.3 1.1 fusion.5
  155.5 3.1 %collective-permute-start.20 = (bf16[96,4096]{1,0:T(8,128)(2,1)}, bf16[96,4096]{1,0:T(8,128)(2,1)}, u32[]{:S(2)}, u32[]{:S(2)}) collective-permute-start(bf16[96,4096]{1,0:T(8,128)(2,1)} %fusion.5), channel_id=1, source_target_pairs={{0,224},{4,228},{8,232},{12,236},{16,240},{20,244},{24,248},{28,25... | collective-permute-start | bytes 2359304 | tf_op jit(solution)/shard_map/ppermute | solution.py:32
  158.6 1.2 select_convert_fusion
  160.6 1.0 mul.60
  161.6 6.3 %collective-permute-done.20 = bf16[96,4096]{1,0:T(8,128)(2,1)} collective-permute-done((bf16[96,4096]{1,0:T(8,128)(2,1)}, bf16[96,4096]{1,0:T(8,128)(2,1)}, u32[]{:S(2)}, u32[]{:S(2)}) %collective-permute-start.20) | collective-permute-done | bytes 786464 | tf_op jit(solution)/shard_map/ppermute | solution.py:32
  167.8 4.5 %collective-permute-done.16 = bf16[96,4096]{1,0:T(8,128)(2,1)} collective-permute-done((bf16[96,4096]{1,0:T(8,128)(2,1)}, bf16[96,4096]{1,0:T(8,128)(2,1)}, u32[]{:S(2)}, u32[]{:S(2)}) %collective-permute-start.16) | collective-permute-done | bytes 786464 | tf_op jit(solution)/shard_map/ppermute | solution.py:32
  172.3 4.0 %fusion.7 = (bf16[96,4096]{1,0:T(8,128)(2,1)S(1)}, f32[96,4096]{1,0:T(8,128)}) fusion(f32[96,4096]{1,0:T(8,128)S(1)} %shard_map.95, bf16[96,4096]{1,0:T(8,128)(2,1)} %copy-done.7, bf16[96,4096]{1,0:T(8,128)(2,1)} %collective-permute-done.16, bf16[96,4096]{1,0:T(8,128)(2,1)} %collective-permute-done.20, f32[96,4096]{1,0:T(8,128)S(1)} %shard_map.91, ...), kind=kLoop, calls=%fused_computation.11 | loop fusion | flops 3932160 | bytes 8650753 | tf_op jit(solution)/shard_map/convert_element_type | solution.py:195
  176.3 0.8 fusion.32
  177.1 1.9 collective-permute-start.21
  179.1 5.5 %collective-permute-start.22 = (bf16[48,4096]{1,0:T(8,128)(2,1)S(1)}, bf16[48,4096]{1,0:T(8,128)(2,1)S(1)}, u32[]{:S(2)}, u32[]{:S(2)}) collective-permute-start(bf16[48,4096]{1,0:T(8,128)(2,1)S(1)} %get-tuple-element.44), channel_id=1, source_target_pairs={{2,194},{6,198},{10,202},{14,206},{18,210},{22,214},{26,218},{30,2... | collective-permute-start | bytes 1179656 | tf_op jit(solution)/shard_map/ppermute | solution.py:32
  184.8 1.1 select_reduce_fusion.1
  186.0 2.7 %collective-permute-start.23 = (bf16[24,4096]{1,0:T(8,128)(2,1)S(1)}, bf16[24,4096]{1,0:T(8,128)(2,1)S(1)}, u32[]{:S(2)}, u32[]{:S(2)}) collective-permute-start(bf16[24,4096]{1,0:T(8,128)(2,1)S(1)} %slice.122), channel_id=1, source_target_pairs={{0,1},{4,5},{8,9},{12,13},{16,17},{20,21},{24,25},{28,29},{1,0},{5... | collective-permute-start | bytes 589832 | tf_op jit(solution)/shard_map/ppermute | solution.py:32
  188.7 9.9 %collective-permute-done.21 = bf16[48,4096]{1,0:T(8,128)(2,1)S(1)} collective-permute-done((bf16[48,4096]{1,0:T(8,128)(2,1)}, bf16[48,4096]{1,0:T(8,128)(2,1)S(1)}, u32[]{:S(2)}, u32[]{:S(2)}) %collective-permute-start.21) | collective-permute-done | bytes 393248 | tf_op jit(solution)/shard_map/ppermute | solution.py:32
  198.6 1.8 collective-permute-done.22
  200.5 2.7 %collective-permute-start.25 = (bf16[24,4096]{1,0:T(8,128)(2,1)S(1)}, bf16[24,4096]{1,0:T(8,128)(2,1)S(1)}, u32[]{:S(2)}, u32[]{:S(2)}) collective-permute-start(bf16[24,4096]{1,0:T(8,128)(2,1)S(1)} %get-tuple-element.42), channel_id=1, source_target_pairs={{0,17},{4,21},{8,25},{12,29},{16,0},{20,4},{24,8},{28,12},{1,16},{... | collective-permute-start | bytes 589832 | tf_op jit(solution)/shard_map/ppermute | solution.py:32
  203.2 3.4 %collective-permute-done.24 = bf16[24,4096]{1,0:T(8,128)(2,1)S(1)} collective-permute-done((bf16[24,4096]{1,0:T(8,128)(2,1)S(1)}, bf16[24,4096]{1,0:T(8,128)(2,1)S(1)}, u32[]{:S(2)}, u32[]{:S(2)}) %collective-permute-start.24) | collective-permute-done | bytes 196640 | tf_op jit(solution)/shard_map/ppermute | solution.py:32
  207.1 26.3 %all_to_all.35 = bf16[24,16,256]{2,0,1:T(8,128)(2,1)S(1)} all-to-all(bf16[24,16,256]{2,0,1:T(8,128)(2,1)S(1)} %bitcast.93), channel_id=1, replica_groups=mesh['seq'=16,'expert'=8,'ffn'=2] {'expert','ffn'}, dimensions={1} | all-to-all | bytes 393216 | tf_op jit(solution)/shard_map/all_to_all | solution.py:255
  233.4 0.9 fusion.10
  (98 shorter events, 10.2 us)
Async XLA Ops:
  0.0 37.3 %copy-start = (bf16[128,256]{1,0:T(8,128)(2,1)S(1)}, bf16[128,256]{1,0:T(8,128)(2,1)}, u32[]{:S(2)}) copy-start(bf16[128,256]{1,0:T(8,128)(2,1)} %param.9) | copy-start | bytes 196612
  0.8 11.2 %copy-start.11 = (s32[128,2]{0,1:T(2,128)S(1)}, s32[128,2]{0,1:T(2,128)}, u32[]{:S(2)}) copy-start(s32[128,2]{0,1:T(2,128)} %param.13) | copy-start | bytes 3076
  1.9 35.4 %all-to-all-start = ((bf16[16,128,256]{2,1,0:T(8,128)(2,1)}), bf16[16,128,256]{2,1,0:T(8,128)(2,1)S(1)}, u32[]{:S(2)}, u32[]{:S(2)}) async-start(bf16[16,128,256]{2,1,0:T(8,128)(2,1)} %broadcast_in_dim.52), calls=%async_computation | async-start | bytes 2097152 | tf_op jit(solution)/shard_map/all_to_all | solution.py:154
  38.2 1.4 copy-start.9
  40.5 19.3 %all-to-all-start.1 = ((bf16[16,24,1,256]{3,1,2,0:T(8,128)(2,1)}), bf16[16,24,1,256]{3,1,2,0:T(8,128)(2,1)S(1)}, u32[]{:S(2)}, u32[]{:S(2)}) async-start(bf16[16,24,1,256]{3,1,2,0:T(8,128)(2,1)} %bitcast.10), calls=%async_computation.1 | async-start | bytes 393216 | tf_op jit(solution)/shard_map/all_to_all | solution.py:174
  59.8 18.7 %copy-start.8 = (bf16[3,8,16,256]{3,1,2,0:T(8,128)(2,1)}, bf16[3,8,16,256]{3,1,2,0:T(8,128)(2,1)S(1)}, u32[]{:S(2)}) copy-start(bf16[3,8,16,256]{3,1,2,0:T(8,128)(2,1)S(1)} %copy.68) | copy-start | bytes 589828
  59.8 14.3 %collective-permute-start.2 = (bf16[24,4096]{1,0:T(8,128)(2,1)S(1)}, bf16[24,4096]{1,0:T(8,128)(2,1)S(1)}, u32[]{:S(2)}, u32[]{:S(2)}) collective-permute-start(bf16[24,4096]{1,0:T(8,128)(2,1)S(1)} %bitcast.84), channel_id=1, source_target_pairs={{0,1},{4,5},{8,9},{12,13},{16,17},{20,21},{24,25},{28,29},{1,0},{5... | collective-permute-start | bytes 589832 | tf_op jit(solution)/shard_map/ppermute | solution.py:32
  61.1 9.6 %collective-permute-start.1 = (bf16[24,4096]{1,0:T(8,128)(2,1)S(1)}, bf16[24,4096]{1,0:T(8,128)(2,1)S(1)}, u32[]{:S(2)}, u32[]{:S(2)}) collective-permute-start(bf16[24,4096]{1,0:T(8,128)(2,1)S(1)} %bitcast.85), channel_id=1, source_target_pairs={{0,16},{4,20},{8,24},{12,28},{16,1},{20,5},{24,9},{28,13},{1,17},{... | collective-permute-start | bytes 589832 | tf_op jit(solution)/shard_map/ppermute | solution.py:32
  61.4 9.2 %collective-permute-start = (bf16[24,4096]{1,0:T(8,128)(2,1)S(1)}, bf16[24,4096]{1,0:T(8,128)(2,1)S(1)}, u32[]{:S(2)}, u32[]{:S(2)}) collective-permute-start(bf16[24,4096]{1,0:T(8,128)(2,1)S(1)} %bitcast.86), channel_id=1, source_target_pairs={{0,17},{4,21},{8,25},{12,29},{16,0},{20,4},{24,8},{28,12},{1,16},{... | collective-permute-start | bytes 589832 | tf_op jit(solution)/shard_map/ppermute | solution.py:32
  70.7 19.2 %collective-permute-start.5 = (bf16[48,4096]{1,0:T(8,128)(2,1)S(1)}, bf16[48,4096]{1,0:T(8,128)(2,1)S(1)}, u32[]{:S(2)}, u32[]{:S(2)}) collective-permute-start(bf16[48,4096]{1,0:T(8,128)(2,1)S(1)} %get-tuple-element.52), channel_id=1, source_target_pairs={{2,194},{6,198},{10,202},{14,206},{18,210},{22,214},{26,218},{30,2... | collective-permute-start | bytes 1179656 | tf_op jit(solution)/shard_map/ppermute | solution.py:32
  74.2 17.2 %collective-permute-start.4 = (bf16[96,4096]{1,0:T(8,128)(2,1)S(1)}, bf16[96,4096]{1,0:T(8,128)(2,1)S(1)}, u32[]{:S(2)}, u32[]{:S(2)}) collective-permute-start(bf16[96,4096]{1,0:T(8,128)(2,1)S(1)} %constant_dynamic-update-slice_fusion.refs_0_), channel_id=1, source_target_pairs={{0,224},{4,228},{8,232},{12,236},{16,240},{20,244},{24,248},{28,25... | collective-permute-start | bytes 2359304 | tf_op jit(solution)/shard_map/ppermute | solution.py:32
  74.2 17.1 %collective-permute-start.3 = (bf16[96,4096]{1,0:T(8,128)(2,1)S(1)}, bf16[96,4096]{1,0:T(8,128)(2,1)S(1)}, u32[]{:S(2)}, u32[]{:S(2)}) collective-permute-start(bf16[96,4096]{1,0:T(8,128)(2,1)S(1)} %constant_dynamic-update-slice_fusion.refs_0_), channel_id=1, source_target_pairs={{0,32},{4,36},{8,40},{12,44},{16,48},{20,52},{24,56},{28,60},{1,33... | collective-permute-start | bytes 2359304 | tf_op jit(solution)/shard_map/ppermute | solution.py:32
  75.7 15.6 %collective-permute-start.6 = (bf16[48,4096]{1,0:T(8,128)(2,1)S(1)}, bf16[48,4096]{1,0:T(8,128)(2,1)S(1)}, u32[]{:S(2)}, u32[]{:S(2)}) collective-permute-start(bf16[48,4096]{1,0:T(8,128)(2,1)S(1)} %get-tuple-element.51), channel_id=1, source_target_pairs={{2,66},{6,70},{10,74},{14,78},{18,82},{22,86},{26,90},{30,94},{3,6... | collective-permute-start | bytes 1179656 | tf_op jit(solution)/shard_map/ppermute | solution.py:32
  78.5 2.0 copy-start.1
  80.6 2.0 copy-start.3
  82.6 2.0 copy-start.4
  91.5 12.4 %collective-permute-start.7 = (bf16[96,4096]{1,0:T(8,128)(2,1)S(1)}, bf16[96,4096]{1,0:T(8,128)(2,1)S(1)}, u32[]{:S(2)}, u32[]{:S(2)}) collective-permute-start(bf16[96,4096]{1,0:T(8,128)(2,1)S(1)} %get-tuple-element.50), channel_id=1, source_target_pairs={{0,32},{4,36},{8,40},{12,44},{16,48},{20,52},{24,56},{28,60},{1,33... | collective-permute-start | bytes 2359304 | tf_op jit(solution)/shard_map/ppermute | solution.py:32
  91.6 12.3 %collective-permute-start.8 = (bf16[96,4096]{1,0:T(8,128)(2,1)S(1)}, bf16[96,4096]{1,0:T(8,128)(2,1)S(1)}, u32[]{:S(2)}, u32[]{:S(2)}) collective-permute-start(bf16[96,4096]{1,0:T(8,128)(2,1)S(1)} %get-tuple-element.49), channel_id=1, source_target_pairs={{0,224},{4,228},{8,232},{12,236},{16,240},{20,244},{24,248},{28,25... | collective-permute-start | bytes 2359304 | tf_op jit(solution)/shard_map/ppermute | solution.py:32
  104.0 12.3 %collective-permute-start.9 = (bf16[96,4096]{1,0:T(8,128)(2,1)S(1)}, bf16[96,4096]{1,0:T(8,128)(2,1)S(1)}, u32[]{:S(2)}, u32[]{:S(2)}) collective-permute-start(bf16[96,4096]{1,0:T(8,128)(2,1)S(1)} %collective-permute-done.7.refs_1_), channel_id=1, source_target_pairs={{0,32},{4,36},{8,40},{12,44},{16,48},{20,52},{24,56},{28,60},{1,33... | collective-permute-start | bytes 2359304 | tf_op jit(solution)/shard_map/ppermute | solution.py:32
  104.0 13.0 %collective-permute-start.10 = (bf16[96,4096]{1,0:T(8,128)(2,1)S(1)}, bf16[96,4096]{1,0:T(8,128)(2,1)S(1)}, u32[]{:S(2)}, u32[]{:S(2)}) collective-permute-start(bf16[96,4096]{1,0:T(8,128)(2,1)S(1)} %broadcast_select_fusion), channel_id=1, source_target_pairs={{0,224},{4,228},{8,232},{12,236},{16,240},{20,244},{24,248},{28,25... | collective-permute-start | bytes 2359304 | tf_op jit(solution)/shard_map/ppermute | solution.py:32
  116.3 7.5 %collective-permute-start.11 = (bf16[48,4096]{1,0:T(8,128)(2,1)S(1)}, bf16[48,4096]{1,0:T(8,128)(2,1)S(1)}, u32[]{:S(2)}, u32[]{:S(2)}) collective-permute-start(bf16[48,4096]{1,0:T(8,128)(2,1)S(1)} %slice.63), channel_id=1, source_target_pairs={{0,32},{4,36},{8,40},{12,44},{16,48},{20,52},{24,56},{28,60},{1,33... | collective-permute-start | bytes 1179656 | tf_op jit(solution)/shard_map/ppermute | solution.py:32
  117.1 6.7 %collective-permute-start.12 = (bf16[48,4096]{1,0:T(8,128)(2,1)S(1)}, bf16[48,4096]{1,0:T(8,128)(2,1)S(1)}, u32[]{:S(2)}, u32[]{:S(2)}) collective-permute-start(bf16[48,4096]{1,0:T(8,128)(2,1)S(1)} %slice.80), channel_id=1, source_target_pairs={{0,224},{4,228},{8,232},{12,236},{16,240},{20,244},{24,248},{28,25... | collective-permute-start | bytes 1179656 | tf_op jit(solution)/shard_map/ppermute | solution.py:32
  117.8 6.2 %copy-start.2 = (bf16[1,4096,448]{1,2,0:T(8,128)(2,1)S(1)}, bf16[1,4096,448]{1,2,0:T(8,128)(2,1)}, u32[]{:S(2)}) copy-start(bf16[1,4096,448]{1,2,0:T(8,128)(2,1)} %param.15) | copy-start | bytes 11010052
  129.5 1.4 collective-permute-start.17
  130.2 2.7 %collective-permute-start.13 = (bf16[48,4096]{1,0:T(8,128)(2,1)S(1)}, bf16[48,4096]{1,0:T(8,128)(2,1)S(1)}, u32[]{:S(2)}, u32[]{:S(2)}) collective-permute-start(bf16[48,4096]{1,0:T(8,128)(2,1)S(1)} %get-tuple-element.47), channel_id=1, source_target_pairs={{0,32},{4,36},{8,40},{12,44},{16,48},{20,52},{24,56},{28,60},{1,33... | collective-permute-start | bytes 1179656 | tf_op jit(solution)/shard_map/ppermute | solution.py:32
  131.0 11.2 %collective-permute-start.18 = (bf16[96,4096]{1,0:T(8,128)(2,1)S(1)}, bf16[96,4096]{1,0:T(8,128)(2,1)S(1)}, u32[]{:S(2)}, u32[]{:S(2)}) collective-permute-start(bf16[96,4096]{1,0:T(8,128)(2,1)S(1)} %add_convert_fusion.1), channel_id=1, source_target_pairs={{0,224},{4,228},{8,232},{12,236},{16,240},{20,244},{24,248},{28,25... | collective-permute-start | bytes 2359304 | tf_op jit(solution)/shard_map/ppermute | solution.py:32
  133.0 12.4 %collective-permute-start.14 = (bf16[96,4096]{1,0:T(8,128)(2,1)S(1)}, bf16[96,4096]{1,0:T(8,128)(2,1)S(1)}, u32[]{:S(2)}, u32[]{:S(2)}) collective-permute-start(bf16[96,4096]{1,0:T(8,128)(2,1)S(1)} %add_convert_fusion.3), channel_id=1, source_target_pairs={{0,32},{4,36},{8,40},{12,44},{16,48},{20,52},{24,56},{28,60},{1,33... | collective-permute-start | bytes 2359304 | tf_op jit(solution)/shard_map/ppermute | solution.py:32
  142.4 12.0 %collective-permute-start.19 = (bf16[96,4096]{1,0:T(8,128)(2,1)S(1)}, bf16[96,4096]{1,0:T(8,128)(2,1)S(1)}, u32[]{:S(2)}, u32[]{:S(2)}) collective-permute-start(bf16[96,4096]{1,0:T(8,128)(2,1)S(1)} %add_convert_fusion), channel_id=1, source_target_pairs={{0,224},{4,228},{8,232},{12,236},{16,240},{20,244},{24,248},{28,25... | collective-permute-start | bytes 2359304 | tf_op jit(solution)/shard_map/ppermute | solution.py:32
  145.7 12.9 %collective-permute-start.15 = (bf16[96,4096]{1,0:T(8,128)(2,1)S(1)}, bf16[96,4096]{1,0:T(8,128)(2,1)S(1)}, u32[]{:S(2)}, u32[]{:S(2)}) collective-permute-start(bf16[96,4096]{1,0:T(8,128)(2,1)S(1)} %add_convert_fusion.2), channel_id=1, source_target_pairs={{0,32},{4,36},{8,40},{12,44},{16,48},{20,52},{24,56},{28,60},{1,33... | collective-permute-start | bytes 2359304 | tf_op jit(solution)/shard_map/ppermute | solution.py:32
  154.3 1.1 copy-start.7
  155.5 12.4 %collective-permute-start.20 = (bf16[96,4096]{1,0:T(8,128)(2,1)}, bf16[96,4096]{1,0:T(8,128)(2,1)}, u32[]{:S(2)}, u32[]{:S(2)}) collective-permute-start(bf16[96,4096]{1,0:T(8,128)(2,1)} %fusion.5), channel_id=1, source_target_pairs={{0,224},{4,228},{8,232},{12,236},{16,240},{20,244},{24,248},{28,25... | collective-permute-start | bytes 2359304 | tf_op jit(solution)/shard_map/ppermute | solution.py:32
  158.6 1.2 copy-start.6
  159.8 12.6 %collective-permute-start.16 = (bf16[96,4096]{1,0:T(8,128)(2,1)}, bf16[96,4096]{1,0:T(8,128)(2,1)}, u32[]{:S(2)}, u32[]{:S(2)}) collective-permute-start(bf16[96,4096]{1,0:T(8,128)(2,1)} %select_convert_fusion), channel_id=1, source_target_pairs={{0,32},{4,36},{8,40},{12,44},{16,48},{20,52},{24,56},{28,60},{1,33... | collective-permute-start | bytes 2359304 | tf_op jit(solution)/shard_map/ppermute | solution.py:32
  176.3 9.6 %copy-start.5 = (f32[96,4096]{1,0:T(8,128)S(1)}, f32[96,4096]{1,0:T(8,128)}, u32[]{:S(2)}) copy-start(f32[96,4096]{1,0:T(8,128)} %get-tuple-element.46) | copy-start | bytes 4718596
  177.1 21.4 %collective-permute-start.21 = (bf16[48,4096]{1,0:T(8,128)(2,1)}, bf16[48,4096]{1,0:T(8,128)(2,1)S(1)}, u32[]{:S(2)}, u32[]{:S(2)}) collective-permute-start(bf16[48,4096]{1,0:T(8,128)(2,1)} %get-tuple-element.43), channel_id=1, source_target_pairs={{2,66},{6,70},{10,74},{14,78},{18,82},{22,86},{26,90},{30,94},{3,6... | collective-permute-start | bytes 1179656 | tf_op jit(solution)/shard_map/ppermute | solution.py:32
  179.1 21.3 %collective-permute-start.22 = (bf16[48,4096]{1,0:T(8,128)(2,1)S(1)}, bf16[48,4096]{1,0:T(8,128)(2,1)S(1)}, u32[]{:S(2)}, u32[]{:S(2)}) collective-permute-start(bf16[48,4096]{1,0:T(8,128)(2,1)S(1)} %get-tuple-element.44), channel_id=1, source_target_pairs={{2,194},{6,198},{10,202},{14,206},{18,210},{22,214},{26,218},{30,2... | collective-permute-start | bytes 1179656 | tf_op jit(solution)/shard_map/ppermute | solution.py:32
  186.0 17.2 %collective-permute-start.23 = (bf16[24,4096]{1,0:T(8,128)(2,1)S(1)}, bf16[24,4096]{1,0:T(8,128)(2,1)S(1)}, u32[]{:S(2)}, u32[]{:S(2)}) collective-permute-start(bf16[24,4096]{1,0:T(8,128)(2,1)S(1)} %slice.122), channel_id=1, source_target_pairs={{0,1},{4,5},{8,9},{12,13},{16,17},{20,21},{24,25},{28,29},{1,0},{5... | collective-permute-start | bytes 589832 | tf_op jit(solution)/shard_map/ppermute | solution.py:32
  200.4 32.9 %copy-start.10 = (bf16[128,256]{1,0:T(8,128)(2,1)S(1)}, bf16[128,256]{1,0:T(8,128)(2,1)}, u32[]{:S(2)}) copy-start(bf16[128,256]{1,0:T(8,128)(2,1)} %param.12) | copy-start | bytes 196612
  200.5 6.2 %collective-permute-start.24 = (bf16[24,4096]{1,0:T(8,128)(2,1)S(1)}, bf16[24,4096]{1,0:T(8,128)(2,1)S(1)}, u32[]{:S(2)}, u32[]{:S(2)}) collective-permute-start(bf16[24,4096]{1,0:T(8,128)(2,1)S(1)} %get-tuple-element.41), channel_id=1, source_target_pairs={{0,16},{4,20},{8,24},{12,28},{16,1},{20,5},{24,9},{28,13},{1,17},{... | collective-permute-start | bytes 589832 | tf_op jit(solution)/shard_map/ppermute | solution.py:32
  200.5 6.4 %collective-permute-start.25 = (bf16[24,4096]{1,0:T(8,128)(2,1)S(1)}, bf16[24,4096]{1,0:T(8,128)(2,1)S(1)}, u32[]{:S(2)}, u32[]{:S(2)}) collective-permute-start(bf16[24,4096]{1,0:T(8,128)(2,1)S(1)} %get-tuple-element.42), channel_id=1, source_target_pairs={{0,17},{4,21},{8,25},{12,29},{16,0},{20,4},{24,8},{28,12},{1,16},{... | collective-permute-start | bytes 589832 | tf_op jit(solution)/shard_map/ppermute | solution.py:32
where the time goes:
time: 235 us; the launch traced here: 234 us
  waiting for transfers between devices  91 us (39%)
  starting transfers between devices  61.9 us (26%)
  Pallas kernels  28.6 us (12%)
  blocking collectives  26.3 us (11%)
  local copies, waits for them, and re-layouts  11.1 us (5%)
  other arithmetic  10.1 us (4%)
  matrix products  4.68 us (2%)
    ppermute x26, waiting for transfers between devices, hop(): return lax.ppermute(value, ALL, pairs)  59.3 us
    ppermute x26, starting transfers between devices, hop(): return lax.ppermute(value, ALL, pairs)  40.9 us
    pallas_call x5, Pallas kernels, expert(): pl.pallas_call(functools.partial(expert_kernel, tuple(places), tuple(outs...  28.6 us
    all_to_all x1, blocking collectives, shards(): lax.all_to_all(back, ('expert', 'ffn'), split_axis=1, concat_axis=0, tile...  26.3 us
    all_to_all x1, waiting for transfers between devices, shards(): lax.all_to_all(jnp.broadcast_to(pair[None], (n_seq,) + pair.shape), 'seq'...  23.5 us
    all_to_all x1, starting transfers between devices, shards(): lax.all_to_all(send, ('expert', 'ffn'), split_axis=0, concat_axis=2, tile...  11 us
    all_to_all x1, starting transfers between devices, shards(): lax.all_to_all(jnp.broadcast_to(pair[None], (n_seq,) + pair.shape), 'seq'...  10 us
    all_to_all x1, waiting for transfers between devices, shards(): lax.all_to_all(send, ('expert', 'ffn'), split_axis=0, concat_axis=2, tile...  8.27 us
  transfers between devices with their start and end apart: 28, of which 14 were waited for; matrix products, arithmetic and copies ran while one was open for 4% of the time, Pallas kernels for 10%

commit v1 on v0

--- a/solution.py
+++ b/solution.py
@@ -203,15 +203,15 @@
     near = [
         hop(rows, (0, -1), (-1, 0)),
         hop(rows, (0, 1), (1, 0)),
-        hop(rows, (0, 2), (4, 0)),
+        hop(rows, (0, 2), (-2, 0)),
     ]
+    below = hop(rows, None, (2, 0))
     own = jnp.concatenate([rows] + near, axis=0)
     plus, minus = [None], [None]
     plus.append(hop(own, (-1, 0), (0, -1)))
     minus.append(hop(own, (1, 0), (0, 1)))
-    next_plus = hop(own[: 2 * n], None, (-2, 0))
-    next_minus = hop(jnp.concatenate([rows, near[1]], axis=0), None, (2, 0))
-    other = jnp.concatenate([next_plus, next_minus], axis=0)
+    wide = [hop(near[2], None, (-1, 0)), hop(below, None, (1, 0)), hop(near[2], None, (-2, 0))]
+    other = jnp.concatenate([below] + wide, axis=0)
     ((sum_own,),) = expert([[own]], *weights)
     sum_own, minus[1] = lax.optimization_barrier((sum_own, minus[1]))
     plus.append(hop(pick(plus[1], other), (-1, 0), (0, -1)))
@@ -227,29 +227,31 @@
     sums[3] = pair(expert([[plus[3]], [minus[3]]], *weights))
     sums[3], far_minus = lax.optimization_barrier((sums[3], far_minus))
     last = pick(jnp.concatenate([far_plus, far_minus], axis=0), other)
+    early = hop(b16(pick(sums[3][1], sums[1][1])), (-1, 0), (0, -1))
     ((sum_last,),) = expert([[last]], *weights)
 
-    turn_plus = hop(b16(sum_last[: 2 * n]), (1, 0), None)
-    turn_minus = hop(b16(sum_last[2 * n :]), (-1, 0), None)
-    go_plus = sums[3][0] + jnp.pad(f32(turn_plus), ((0, 2 * n), (0, 0)))
-    go_minus = sums[3][1] + jnp.pad(f32(turn_minus), ((2 * n, 0), (0, 0)))
-    plus_2, minus_2 = hop(b16(go_plus), (1, 0), (0, 1)), hop(b16(go_minus), (-1, 0), (0, -1))
-    go_plus = pick(sums[2][0], sums[1][0]) + f32(plus_2)
-    go_minus = sums[2][1] + f32(minus_2)
-    plus_3, minus_3 = hop(b16(go_plus), (1, 0), (0, 1)), hop(b16(go_minus), (-1, 0), (0, -1))
-    go_plus = pick(sums[1][0] + f32(plus_3), sums[2][0])
-    go_minus = sums[1][1] + pick(f32(minus_3), 0.0)
-    plus_4, minus_4 = hop(b16(go_plus), (1, 0), (0, 1)), hop(b16(go_minus), (-1, 0), (0, -1))
-    total = sum_own + f32(pick(plus_4, plus_3)) + f32(minus_4)
-    rest = b16(sum_last + f32(minus_3) + f32(plus_4))
-    from_minus, from_plus = hop(rest[: 2 * n], None, (2, 0)), hop(rest[2 * n :], None, (-2, 0))
+    plus_1, minus_1 = hop(b16(pick(sum_last, sums[3][1])), (1, 0), (0, 1)), early
+    go_minus = sums[2][1] + pick(f32(minus_1), 0.0)
+    minus_2 = hop(b16(go_minus), (-1, 0), (0, -1))
+    go_plus = pick(sums[3][0], sums[2][0]) + f32(plus_1)
+    plus_2 = hop(b16(go_plus), (1, 0), (0, 1))
+    minus_3 = hop(b16(sums[1][1] + f32(minus_2)), (-1, 0), None)
+    plus_3 = hop(b16(pick(sums[2][0] + f32(plus_2), sums[3][0])), (1, 0), (0, 1))
+    both = lax.optimization_barrier((plus_2, minus_2))
+    rest = sum_last + f32(both[0]) + f32(both[1])
+    rest = [rest[k * n : (k + 1) * n] for k in range(4)]
+    from_1, from_2 = hop(b16(rest[1]), None, (1, 0)), hop(b16(rest[3]), None, (2, 0))
+    from_above = hop(b16(rest[2]), None, (-1, 0))
+    from_1, from_2, from_above, _ = lax.optimization_barrier((from_1, from_2, from_above, plus_3))
+    plus_4 = hop(b16(sums[1][0] + f32(plus_3)), (1, 0), (0, 1))
+    last_down = hop(b16(rest[0] + f32(from_above)), None, (-2, 0))
+    last_down, plus_4 = lax.optimization_barrier((last_down, plus_4))
+    total = sum_own + f32(plus_4) + f32(pick(minus_3, minus_1))
     chunk = [total[k * n : (k + 1) * n] for k in range(4)]
-    chunk_1 = chunk[1] + f32(from_minus[n:])
-    chunk_2 = chunk[2] + f32(from_plus[n:])
-    result = chunk[0] + f32(from_minus[:n]) + f32(from_plus[:n])
-    result = result + f32(hop(b16(chunk[3]), (0, 2), (4, 0)))
-    result = result + f32(hop(b16(chunk_1), (0, 1), (1, 0)))
-    result = result + f32(hop(b16(chunk_2), (0, -1), (-1, 0)))
+    result = chunk[0] + f32(last_down)
+    result = result + f32(hop(b16(chunk[1]), (0, 1), (1, 0)))
+    result = result + f32(hop(b16(chunk[2]), (0, -1), (-1, 0)))
+    result = result + f32(hop(b16(chunk[3] + f32(from_1) + f32(from_2)), (0, 2), (2, 0)))
 
     back = (result * weight[:, None]).astype(jnp.bfloat16).reshape(half_cap, n_exp * n_ffn, span)
     returned = lax.all_to_all(

time: 235 us -> 220 us (0.936)
  blocking collectives: 26.3 us -> 16.4 us
  waiting for transfers between devices: 91 us -> 82.4 us
  starting transfers between devices: 61.9 us -> 67.5 us
  other arithmetic: 10.1 us -> 7.33 us
    all_to_all x1, blocking collectives: 26.3 us -> 16.4 us  [shards(): lax.all_to_all(back, ('expert', 'ffn'), split_axis=1, concat_axis=0, tile...]
    ppermute x26 -> x29, waiting for transfers between devices: 59.3 us -> 50.7 us  [hop(): return lax.ppermute(value, ALL, pairs)]
    ppermute x26 -> x29, starting transfers between devices: 40.9 us -> 46.5 us  [hop(): return lax.ppermute(value, ALL, pairs)]
    convert_element_type x8, other arithmetic: 7.01 us -> 3.73 us  [b16(): return v.astype(jnp.bfloat16)]
    unnamed x30 -> x50, local copies, waits for them, and re-layouts: 6.35 us -> 8.43 us
  transfers between devices with their start and end apart: 28 -> 31, of which waited for: 14 -> 13; matrix products, arithmetic and copies ran while one was open for 4% -> 3% of each run, Pallas kernels for 10% -> 11%
where the time goes in v1:
time: 220 us; the launch traced here: 219 us
  waiting for transfers between devices  82.4 us (37%)
  starting transfers between devices  67.5 us (31%)
  Pallas kernels  28.5 us (13%)
  blocking collectives  16.4 us (7%)
  local copies, waits for them, and re-layouts  12.3 us (6%)
  other arithmetic  7.33 us (3%)
  matrix products  3.76 us (2%)
    ppermute x29, waiting for transfers between devices, hop(): return lax.ppermute(value, ALL, pairs)  50.7 us
    ppermute x29, starting transfers between devices, hop(): return lax.ppermute(value, ALL, pairs)  46.5 us
    pallas_call x5, Pallas kernels, expert(): pl.pallas_call(functools.partial(expert_kernel, tuple(places), tuple(outs...  28.5 us
    all_to_all x1, waiting for transfers between devices, shards(): lax.all_to_all(jnp.broadcast_to(pair[None], (n_seq,) + pair.shape), 'seq'...  23.5 us
    all_to_all x1, blocking collectives, shards(): lax.all_to_all(back, ('expert', 'ffn'), split_axis=1, concat_axis=0, tile...  16.4 us
    all_to_all x1, starting transfers between devices, shards(): lax.all_to_all(send, ('expert', 'ffn'), split_axis=0, concat_axis=2, tile...  11 us
    all_to_all x1, starting transfers between devices, shards(): lax.all_to_all(jnp.broadcast_to(pair[None], (n_seq,) + pair.shape), 'seq'...  10 us
    unnamed x50, local copies, waits for them, and re-layouts  8.43 us
  transfers between devices with their start and end apart: 31, of which 13 were waited for; matrix products, arithmetic and copies ran while one was open for 3% of the time, Pallas kernels for 11%

profile of v1, /device:TPU:1, one launch (start us, length us, event | category | flops | bytes accessed | tf_op | source)
XLA Modules:
  0.0 219.1 jit_solution(4557924483838553660)
XLA Ops:
  0.8 1.1 broadcast_in_dim.52
  1.9 10.0 %all-to-all-start = ((bf16[16,128,256]{2,1,0:T(8,128)(2,1)}), bf16[16,128,256]{2,1,0:T(8,128)(2,1)S(1)}, u32[]{:S(2)}, u32[]{:S(2)}) async-start(bf16[16,128,256]{2,1,0:T(8,128)(2,1)} %broadcast_in_dim.52), calls=%async_computation | async-start | bytes 2097152 | tf_op jit(solution)/shard_map/all_to_all | solution.py:154
  13.8 23.5 %all-to-all-done = bf16[16,128,256]{2,1,0:T(8,128)(2,1)S(1)} async-done(((bf16[16,128,256]{2,1,0:T(8,128)(2,1)}), bf16[16,128,256]{2,1,0:T(8,128)(2,1)S(1)}, u32[]{:S(2)}, u32[]{:S(2)}) %all-to-all-start) | async-done | bytes 1048608 | tf_op jit(solution)/shard_map/all_to_all | solution.py:154
  38.2 1.3 fusion.5
  39.7 0.9 convolution_convert_fusion
  40.5 11.0 %all-to-all-start.1 = ((bf16[16,24,1,256]{3,1,2,0:T(8,128)(2,1)}), bf16[16,24,1,256]{3,1,2,0:T(8,128)(2,1)S(1)}, u32[]{:S(2)}, u32[]{:S(2)}) async-start(bf16[16,24,1,256]{3,1,2,0:T(8,128)(2,1)} %bitcast.10), calls=%async_computation.1 | async-start | bytes 393216 | tf_op jit(solution)/shard_map/all_to_all | solution.py:174
  51.5 8.3 %all-to-all-done.1 = bf16[16,24,1,256]{3,1,2,0:T(8,128)(2,1)S(1)} async-done(((bf16[16,24,1,256]{3,1,2,0:T(8,128)(2,1)}), bf16[16,24,1,256]{3,1,2,0:T(8,128)(2,1)S(1)}, u32[]{:S(2)}, u32[]{:S(2)}) %all-to-all-start.1) | async-done | bytes 196640 | tf_op jit(solution)/shard_map/all_to_all | solution.py:174
  59.8 2.0 collective-permute-start.5
  61.9 3.5 %collective-permute-start.2 = (bf16[24,4096]{1,0:T(8,128)(2,1)S(1)}, bf16[24,4096]{1,0:T(8,128)(2,1)S(1)}, u32[]{:S(2)}, u32[]{:S(2)}) collective-permute-start(bf16[24,4096]{1,0:T(8,128)(2,1)S(1)} %bitcast.88), channel_id=1, source_target_pairs={{0,1},{4,5},{8,9},{12,13},{16,17},{20,21},{24,25},{28,29},{1,0},{5... | collective-permute-start | bytes 589832 | tf_op jit(solution)/shard_map/ppermute | solution.py:32
  65.4 2.7 %collective-permute-start = (bf16[24,4096]{1,0:T(8,128)(2,1)S(1)}, bf16[24,4096]{1,0:T(8,128)(2,1)S(1)}, u32[]{:S(2)}, u32[]{:S(2)}) collective-permute-start(bf16[24,4096]{1,0:T(8,128)(2,1)S(1)} %bitcast.90), channel_id=1, source_target_pairs={{0,17},{4,21},{8,25},{12,29},{16,0},{20,4},{24,8},{28,12},{1,16},{... | collective-permute-start | bytes 589832 | tf_op jit(solution)/shard_map/ppermute | solution.py:32
  68.1 3.6 %collective-permute-done = bf16[24,4096]{1,0:T(8,128)(2,1)S(1)} collective-permute-done((bf16[24,4096]{1,0:T(8,128)(2,1)S(1)}, bf16[24,4096]{1,0:T(8,128)(2,1)S(1)}, u32[]{:S(2)}, u32[]{:S(2)}) %collective-permute-start) | collective-permute-done | bytes 196640 | tf_op jit(solution)/shard_map/ppermute | solution.py:32
  71.9 1.5 collective-permute-start.3
  73.3 5.1 %collective-permute-start.8 = (bf16[24,4096]{1,0:T(8,128)(2,1)S(1)}, bf16[24,4096]{1,0:T(8,128)(2,1)S(1)}, u32[]{:S(2)}, u32[]{:S(2)}) collective-permute-start(bf16[24,4096]{1,0:T(8,128)(2,1)S(1)} %collective-permute-done.2), channel_id=1, source_target_pairs={{2,194},{6,198},{10,202},{14,206},{18,210},{22,214},{26,218},{30,2... | collective-permute-start | bytes 589832 | tf_op jit(solution)/shard_map/ppermute | solution.py:32
  78.5 2.1 collective-permute-start.6
  80.6 3.2 %collective-permute-start.7 = (bf16[24,4096]{1,0:T(8,128)(2,1)S(1)}, bf16[24,4096]{1,0:T(8,128)(2,1)S(1)}, u32[]{:S(2)}, u32[]{:S(2)}) collective-permute-start(bf16[24,4096]{1,0:T(8,128)(2,1)S(1)} %collective-permute-done.5), channel_id=1, source_target_pairs={{2,34},{6,38},{10,42},{14,46},{18,50},{22,54},{26,58},{30,62},{3,3... | collective-permute-start | bytes 589832 | tf_op jit(solution)/shard_map/ppermute | solution.py:32
  83.8 2.0 copy-done.1
  85.8 2.0 copy-done.3
  87.9 2.0 copy-done.4
  89.9 5.3 %shard_map.91 = f32[96,4096]{1,0:T(8,128)S(1)} custom-call(bf16[96,4096]{1,0:T(8,128)(2,1)S(1)} %constant_dynamic-update-slice_fusion.refs_0_, bf16[448,4096]{1,0:T(8,128)(2,1)S(1)} %bitcast.69, bf16[448,4096]{1,0:T(8,128)(2,1)S(1)} %bitcast.74, bf16[448,4096]{1,0:T(8,128)(2,1)S(1)} %bitcast.79), custom_call_target="tpu_custom_call" | custom-call | flops 1056964608 | bytes 13369344 | tf_op jit(solution)/shard_map/pallas_call | solution.py:98
  95.5 0.9 copy-done.7
  96.4 2.7 %collective-permute-start.9 = (bf16[96,4096]{1,0:T(8,128)(2,1)S(1)}, bf16[96,4096]{1,0:T(8,128)(2,1)S(1)}, u32[]{:S(2)}, u32[]{:S(2)}) collective-permute-start(bf16[96,4096]{1,0:T(8,128)(2,1)S(1)} %get-tuple-element.66), channel_id=1, source_target_pairs={{0,224},{4,228},{8,232},{12,236},{16,240},{20,244},{24,248},{28,25... | collective-permute-start | bytes 2359304 | tf_op jit(solution)/shard_map/ppermute | solution.py:32
  99.1 6.0 %shard_map.92 = (f32[96,4096]{1,0:T(8,128)S(1)}, f32[96,4096]{1,0:T(8,128)S(1)}) custom-call(bf16[96,4096]{1,0:T(8,128)(2,1)S(1)} %collective-permute-done.4.refs_0_, bf16[96,4096]{1,0:T(8,128)(2,1)S(1)} %collective-permute-done.3.refs_1_, bf16[448,4096]{1,0:T(8,128)(2,1)S(1)} %bitcast.70, bf16[448,4096]{1,0:T(8,128)(2,1)S(1)} %bitcast.75, ...), custom_call_target="tpu_custom_call" | custom-call | flops 2113929216 | bytes 15728640 | tf_op jit(solution)/shard_map/pallas_call | solution.py:98
  105.1 1.1 copy-done.11
  106.2 2.5 %collective-permute-done.12.refs_1_ = bf16[96,4096]{1,0:T(8,128)(2,1)S(1)} collective-permute-done((bf16[96,4096]{1,0:T(8,128)(2,1)S(1)}, bf16[96,4096]{1,0:T(8,128)(2,1)S(1)}, u32[]{:S(2)}, u32[]{:S(2)}) %collective-permute-start.12) | collective-permute-done | bytes 786464 | tf_op jit(solution)/shard_map/ppermute | solution.py:32
  108.9 2.8 %collective-permute-start.10 = (bf16[96,4096]{1,0:T(8,128)(2,1)S(1)}, bf16[96,4096]{1,0:T(8,128)(2,1)S(1)}, u32[]{:S(2)}, u32[]{:S(2)}) collective-permute-start(bf16[96,4096]{1,0:T(8,128)(2,1)S(1)} %broadcast_select_fusion.1), channel_id=1, source_target_pairs={{0,224},{4,228},{8,232},{12,236},{16,240},{20,244},{24,248},{28,25... | collective-permute-start | bytes 2359304 | tf_op jit(solution)/shard_map/ppermute | solution.py:32
  111.6 6.0 %shard_map.93 = (f32[96,4096]{1,0:T(8,128)S(1)}, f32[96,4096]{1,0:T(8,128)S(1)}) custom-call(bf16[96,4096]{1,0:T(8,128)(2,1)S(1)} %collective-permute-done.9.refs_0_, bf16[96,4096]{1,0:T(8,128)(2,1)S(1)} %collective-permute-done.12.refs_1_, bf16[448,4096]{1,0:T(8,128)(2,1)S(1)} %bitcast.71, bf16[448,4096]{1,0:T(8,128)(2,1)S(1)} %bitcast.76, ...), custom_call_target="tpu_custom_call" | custom-call | flops 2113929216 | bytes 15728640 | tf_op jit(solution)/shard_map/pallas_call | solution.py:98
  117.6 3.5 %collective-permute-done.13.refs_1_ = bf16[96,4096]{1,0:T(8,128)(2,1)S(1)} collective-permute-done((bf16[96,4096]{1,0:T(8,128)(2,1)S(1)}, bf16[96,4096]{1,0:T(8,128)(2,1)S(1)}, u32[]{:S(2)}, u32[]{:S(2)}) %collective-permute-start.13) | collective-permute-done | bytes 786464 | tf_op jit(solution)/shard_map/ppermute | solution.py:32
  122.6 6.0 %shard_map.94 = (f32[96,4096]{1,0:T(8,128)S(1)}, f32[96,4096]{1,0:T(8,128)S(1)}) custom-call(bf16[96,4096]{1,0:T(8,128)(2,1)S(1)} %collective-permute-done.10.refs_0_, bf16[96,4096]{1,0:T(8,128)(2,1)S(1)} %collective-permute-done.13.refs_1_, bf16[448,4096]{1,0:T(8,128)(2,1)S(1)} %bitcast.72, bf16[448,4096]{1,0:T(8,128)(2,1)S(1)} %bitcast.77, ...), custom_call_target="tpu_custom_call" | custom-call | flops 2113929216 | bytes 15728640 | tf_op jit(solution)/shard_map/pallas_call | solution.py:98
  128.8 5.3 %shard_map.95 = f32[96,4096]{1,0:T(8,128)S(1)} custom-call(bf16[96,4096]{1,0:T(8,128)(2,1)S(1)} %maximum_select_fusion.refs_0_, bf16[448,4096]{1,0:T(8,128)(2,1)S(1)} %bitcast.73, bf16[448,4096]{1,0:T(8,128)(2,1)S(1)} %bitcast.78, bf16[448,4096]{1,0:T(8,128)(2,1)S(1)} %bitcast.83), custom_call_target="tpu_custom_call" | custom-call | flops 1056964608 | bytes 13369344 | tf_op jit(solution)/shard_map/pallas_call | solution.py:98
  134.2 1.5 select_convert_fusion.2
  136.4 1.0 mul.60
  137.7 2.8 %collective-permute-start.17 = (bf16[96,4096]{1,0:T(8,128)(2,1)}, bf16[96,4096]{1,0:T(8,128)(2,1)S(1)}, u32[]{:S(2)}, u32[]{:S(2)}) collective-permute-start(bf16[96,4096]{1,0:T(8,128)(2,1)} %get-tuple-element.60), channel_id=1, source_target_pairs={{0,224},{4,228},{8,232},{12,236},{16,240},{20,244},{24,248},{28,25... | collective-permute-start | bytes 2359304 | tf_op jit(solution)/shard_map/ppermute | solution.py:32
  140.4 7.6 %collective-permute-done.15 = bf16[96,4096]{1,0:T(8,128)(2,1)} collective-permute-done((bf16[96,4096]{1,0:T(8,128)(2,1)}, bf16[96,4096]{1,0:T(8,128)(2,1)}, u32[]{:S(2)}, u32[]{:S(2)}) %collective-permute-start.15) | collective-permute-done | bytes 786464 | tf_op jit(solution)/shard_map/ppermute | solution.py:32
  148.0 1.3 add_convert_fusion.3
  149.9 3.1 %collective-permute-start.18 = (bf16[96,4096]{1,0:T(8,128)(2,1)S(1)}, bf16[96,4096]{1,0:T(8,128)(2,1)S(1)}, u32[]{:S(2)}, u32[]{:S(2)}) collective-permute-start(bf16[96,4096]{1,0:T(8,128)(2,1)S(1)} %add_convert_fusion.2), channel_id=1, source_target_pairs={{0,224},{4,228},{8,232},{12,236},{16,240},{20,244},{24,248},{28,25... | collective-permute-start | bytes 2359304 | tf_op jit(solution)/shard_map/ppermute | solution.py:32
  153.0 9.0 %collective-permute-done.16 = bf16[96,4096]{1,0:T(8,128)(2,1)S(1)} collective-permute-done((bf16[96,4096]{1,0:T(8,128)(2,1)S(1)}, bf16[96,4096]{1,0:T(8,128)(2,1)S(1)}, u32[]{:S(2)}, u32[]{:S(2)}) %collective-permute-start.16) | collective-permute-done | bytes 786464 | tf_op jit(solution)/shard_map/ppermute | solution.py:32
  162.8 3.3 %collective-permute-start.21 = (bf16[24,4096]{1,0:T(8,128)(2,1)S(1)}, bf16[24,4096]{1,0:T(8,128)(2,1)S(1)}, u32[]{:S(2)}, u32[]{:S(2)}) collective-permute-start(bf16[24,4096]{1,0:T(8,128)(2,1)S(1)} %get-tuple-element.63), channel_id=1, source_target_pairs={{2,226},{6,230},{10,234},{14,238},{18,242},{22,246},{26,250},{30,2... | collective-permute-start | bytes 589832 | tf_op jit(solution)/shard_map/ppermute | solution.py:32
  166.1 2.3 %collective-permute-start.20 = (bf16[24,4096]{1,0:T(8,128)(2,1)S(1)}, bf16[24,4096]{1,0:T(8,128)(2,1)S(1)}, u32[]{:S(2)}, u32[]{:S(2)}) collective-permute-start(bf16[24,4096]{1,0:T(8,128)(2,1)S(1)} %get-tuple-element.64), channel_id=1, source_target_pairs={{2,66},{6,70},{10,74},{14,78},{18,82},{22,86},{26,90},{30,94},{3,6... | collective-permute-start | bytes 589832 | tf_op jit(solution)/shard_map/ppermute | solution.py:32
  168.4 2.1 collective-permute-start.19
  171.5 3.2 %collective-permute-done.22 = bf16[96,4096]{1,0:T(8,128)(2,1)S(1)} collective-permute-done((bf16[96,4096]{1,0:T(8,128)(2,1)S(1)}, bf16[96,4096]{1,0:T(8,128)(2,1)S(1)}, u32[]{:S(2)}, u32[]{:S(2)}) %collective-permute-start.22) | collective-permute-done | bytes 786464 | tf_op jit(solution)/shard_map/ppermute | solution.py:32
  175.0 3.5 %collective-permute-done.20 = bf16[24,4096]{1,0:T(8,128)(2,1)S(1)} collective-permute-done((bf16[24,4096]{1,0:T(8,128)(2,1)S(1)}, bf16[24,4096]{1,0:T(8,128)(2,1)S(1)}, u32[]{:S(2)}, u32[]{:S(2)}) %collective-permute-start.20) | collective-permute-done | bytes 196640 | tf_op jit(solution)/shard_map/ppermute | solution.py:32
  178.5 3.3 %collective-permute-done.19 = bf16[24,4096]{1,0:T(8,128)(2,1)S(1)} collective-permute-done((bf16[24,4096]{1,0:T(8,128)(2,1)S(1)}, bf16[24,4096]{1,0:T(8,128)(2,1)S(1)}, u32[]{:S(2)}, u32[]{:S(2)}) %collective-permute-start.19) | collective-permute-done | bytes 196640 | tf_op jit(solution)/shard_map/ppermute | solution.py:32
  181.8 1.9 collective-permute-start.23
  184.0 6.1 %collective-permute-done.23 = bf16[24,4096]{1,0:T(8,128)(2,1)S(1)} collective-permute-done((bf16[24,4096]{1,0:T(8,128)(2,1)S(1)}, bf16[24,4096]{1,0:T(8,128)(2,1)S(1)}, u32[]{:S(2)}, u32[]{:S(2)}) %collective-permute-start.23) | collective-permute-done | bytes 196640 | tf_op jit(solution)/shard_map/ppermute | solution.py:32
  190.6 2.7 %collective-permute-start.27 = (bf16[24,4096]{1,0:T(8,128)(2,1)S(1)}, bf16[24,4096]{1,0:T(8,128)(2,1)S(1)}, u32[]{:S(2)}, u32[]{:S(2)}) collective-permute-start(bf16[24,4096]{1,0:T(8,128)(2,1)S(1)} %get-tuple-element.62), channel_id=1, source_target_pairs={{0,17},{4,21},{8,25},{12,29},{16,0},{20,4},{24,8},{28,12},{1,16},{... | collective-permute-start | bytes 589832 | tf_op jit(solution)/shard_map/ppermute | solution.py:32
  193.5 3.5 %collective-permute-done.26 = bf16[24,4096]{1,0:T(8,128)(2,1)S(1)} collective-permute-done((bf16[24,4096]{1,0:T(8,128)(2,1)S(1)}, bf16[24,4096]{1,0:T(8,128)(2,1)S(1)}, u32[]{:S(2)}, u32[]{:S(2)}) %collective-permute-start.26) | collective-permute-done | bytes 196640 | tf_op jit(solution)/shard_map/ppermute | solution.py:32
  197.0 4.7 %collective-permute-done.28 = bf16[24,4096]{1,0:T(8,128)(2,1)S(1)} collective-permute-done((bf16[24,4096]{1,0:T(8,128)(2,1)S(1)}, bf16[24,4096]{1,0:T(8,128)(2,1)S(1)}, u32[]{:S(2)}, u32[]{:S(2)}) %collective-permute-start.28) | collective-permute-done | bytes 196640 | tf_op jit(solution)/shard_map/ppermute | solution.py:32
  201.9 16.4 %all_to_all.35 = bf16[24,16,256]{2,0,1:T(8,128)(2,1)S(1)} all-to-all(bf16[24,16,256]{2,0,1:T(8,128)(2,1)S(1)} %bitcast.94), channel_id=1, replica_groups=mesh['seq'=16,'expert'=8,'ffn'=2] {'expert','ffn'}, dimensions={1} | all-to-all | bytes 393216 | tf_op jit(solution)/shard_map/all_to_all | solution.py:257
  (123 shorter events, 11.2 us)
Async XLA Ops:
  0.0 37.3 %copy-start = (bf16[128,256]{1,0:T(8,128)(2,1)S(1)}, bf16[128,256]{1,0:T(8,128)(2,1)}, u32[]{:S(2)}) copy-start(bf16[128,256]{1,0:T(8,128)(2,1)} %param.9) | copy-start | bytes 196612
  0.8 11.2 %copy-start.19 = (s32[128,2]{0,1:T(2,128)S(1)}, s32[128,2]{0,1:T(2,128)}, u32[]{:S(2)}) copy-start(s32[128,2]{0,1:T(2,128)} %param.13) | copy-start | bytes 3076
  1.9 35.4 %all-to-all-start = ((bf16[16,128,256]{2,1,0:T(8,128)(2,1)}), bf16[16,128,256]{2,1,0:T(8,128)(2,1)S(1)}, u32[]{:S(2)}, u32[]{:S(2)}) async-start(bf16[16,128,256]{2,1,0:T(8,128)(2,1)} %broadcast_in_dim.52), calls=%async_computation | async-start | bytes 2097152 | tf_op jit(solution)/shard_map/all_to_all | solution.py:154
  40.5 19.2 %all-to-all-start.1 = ((bf16[16,24,1,256]{3,1,2,0:T(8,128)(2,1)}), bf16[16,24,1,256]{3,1,2,0:T(8,128)(2,1)S(1)}, u32[]{:S(2)}, u32[]{:S(2)}) async-start(bf16[16,24,1,256]{3,1,2,0:T(8,128)(2,1)} %bitcast.10), calls=%async_computation.1 | async-start | bytes 393216 | tf_op jit(solution)/shard_map/all_to_all | solution.py:174
  59.8 35.4 %copy-start.15 = (bf16[3,8,16,256]{3,1,2,0:T(8,128)(2,1)}, bf16[3,8,16,256]{3,1,2,0:T(8,128)(2,1)S(1)}, u32[]{:S(2)}) copy-start(bf16[3,8,16,256]{3,1,2,0:T(8,128)(2,1)S(1)} %copy.68) | copy-start | bytes 589828
  59.8 20.7 %collective-permute-start.5 = (bf16[24,4096]{1,0:T(8,128)(2,1)S(1)}, bf16[24,4096]{1,0:T(8,128)(2,1)S(1)}, u32[]{:S(2)}, u32[]{:S(2)}) collective-permute-start(bf16[24,4096]{1,0:T(8,128)(2,1)S(1)} %bitcast.87), channel_id=1, source_target_pairs={{2,66},{6,70},{10,74},{14,78},{18,82},{22,86},{26,90},{30,94},{3,6... | collective-permute-start | bytes 589832 | tf_op jit(solution)/shard_map/ppermute | solution.py:32
  61.9 9.9 %collective-permute-start.2 = (bf16[24,4096]{1,0:T(8,128)(2,1)S(1)}, bf16[24,4096]{1,0:T(8,128)(2,1)S(1)}, u32[]{:S(2)}, u32[]{:S(2)}) collective-permute-start(bf16[24,4096]{1,0:T(8,128)(2,1)S(1)} %bitcast.88), channel_id=1, source_target_pairs={{0,1},{4,5},{8,9},{12,13},{16,17},{20,21},{24,25},{28,29},{1,0},{5... | collective-permute-start | bytes 589832 | tf_op jit(solution)/shard_map/ppermute | solution.py:32
  65.4 6.3 %collective-permute-start.1 = (bf16[24,4096]{1,0:T(8,128)(2,1)S(1)}, bf16[24,4096]{1,0:T(8,128)(2,1)S(1)}, u32[]{:S(2)}, u32[]{:S(2)}) collective-permute-start(bf16[24,4096]{1,0:T(8,128)(2,1)S(1)} %bitcast.89), channel_id=1, source_target_pairs={{0,16},{4,20},{8,24},{12,28},{16,1},{20,5},{24,9},{28,13},{1,17},{... | collective-permute-start | bytes 589832 | tf_op jit(solution)/shard_map/ppermute | solution.py:32
  65.4 6.3 %collective-permute-start = (bf16[24,4096]{1,0:T(8,128)(2,1)S(1)}, bf16[24,4096]{1,0:T(8,128)(2,1)S(1)}, u32[]{:S(2)}, u32[]{:S(2)}) collective-permute-start(bf16[24,4096]{1,0:T(8,128)(2,1)S(1)} %bitcast.90), channel_id=1, source_target_pairs={{0,17},{4,21},{8,25},{12,29},{16,0},{20,4},{24,8},{28,12},{1,16},{... | collective-permute-start | bytes 589832 | tf_op jit(solution)/shard_map/ppermute | solution.py:32
  71.8 23.6 %collective-permute-start.4 = (bf16[96,4096]{1,0:T(8,128)(2,1)S(1)}, bf16[96,4096]{1,0:T(8,128)(2,1)S(1)}, u32[]{:S(2)}, u32[]{:S(2)}) collective-permute-start(bf16[96,4096]{1,0:T(8,128)(2,1)S(1)} %constant_dynamic-update-slice_fusion.refs_0_), channel_id=1, source_target_pairs={{0,224},{4,228},{8,232},{12,236},{16,240},{20,244},{24,248},{28,25... | collective-permute-start | bytes 2359304 | tf_op jit(solution)/shard_map/ppermute | solution.py:32
  71.9 23.5 %collective-permute-start.3 = (bf16[96,4096]{1,0:T(8,128)(2,1)S(1)}, bf16[96,4096]{1,0:T(8,128)(2,1)S(1)}, u32[]{:S(2)}, u32[]{:S(2)}) collective-permute-start(bf16[96,4096]{1,0:T(8,128)(2,1)S(1)} %constant_dynamic-update-slice_fusion.refs_0_), channel_id=1, source_target_pairs={{0,32},{4,36},{8,40},{12,44},{16,48},{20,52},{24,56},{28,60},{1,33... | collective-permute-start | bytes 2359304 | tf_op jit(solution)/shard_map/ppermute | solution.py:32
  73.3 22.0 %collective-permute-start.8 = (bf16[24,4096]{1,0:T(8,128)(2,1)S(1)}, bf16[24,4096]{1,0:T(8,128)(2,1)S(1)}, u32[]{:S(2)}, u32[]{:S(2)}) collective-permute-start(bf16[24,4096]{1,0:T(8,128)(2,1)S(1)} %collective-permute-done.2), channel_id=1, source_target_pairs={{2,194},{6,198},{10,202},{14,206},{18,210},{22,214},{26,218},{30,2... | collective-permute-start | bytes 589832 | tf_op jit(solution)/shard_map/ppermute | solution.py:32
  78.5 16.8 %collective-permute-start.6 = (bf16[24,4096]{1,0:T(8,128)(2,1)S(1)}, bf16[24,4096]{1,0:T(8,128)(2,1)S(1)}, u32[]{:S(2)}, u32[]{:S(2)}) collective-permute-start(bf16[24,4096]{1,0:T(8,128)(2,1)S(1)} %collective-permute-done.2), channel_id=1, source_target_pairs={{2,226},{6,230},{10,234},{14,238},{18,242},{22,246},{26,250},{30,2... | collective-permute-start | bytes 589832 | tf_op jit(solution)/shard_map/ppermute | solution.py:32
  80.6 14.7 %collective-permute-start.7 = (bf16[24,4096]{1,0:T(8,128)(2,1)S(1)}, bf16[24,4096]{1,0:T(8,128)(2,1)S(1)}, u32[]{:S(2)}, u32[]{:S(2)}) collective-permute-start(bf16[24,4096]{1,0:T(8,128)(2,1)S(1)} %collective-permute-done.5), channel_id=1, source_target_pairs={{2,34},{6,38},{10,42},{14,46},{18,50},{22,54},{26,58},{30,62},{3,3... | collective-permute-start | bytes 589832 | tf_op jit(solution)/shard_map/ppermute | solution.py:32
  83.8 2.0 copy-start.1
  85.8 2.0 copy-start.3
  95.3 3.7 %copy-start.2 = (bf16[1,4096,448]{1,2,0:T(8,128)(2,1)S(1)}, bf16[1,4096,448]{1,2,0:T(8,128)(2,1)}, u32[]{:S(2)}) copy-start(bf16[1,4096,448]{1,2,0:T(8,128)(2,1)} %param.15) | copy-start | bytes 11010052
  96.4 12.3 %collective-permute-start.12 = (bf16[96,4096]{1,0:T(8,128)(2,1)S(1)}, bf16[96,4096]{1,0:T(8,128)(2,1)S(1)}, u32[]{:S(2)}, u32[]{:S(2)}) collective-permute-start(bf16[96,4096]{1,0:T(8,128)(2,1)S(1)} %get-tuple-element.67), channel_id=1, source_target_pairs={{0,32},{4,36},{8,40},{12,44},{16,48},{20,52},{24,56},{28,60},{1,33... | collective-permute-start | bytes 2359304 | tf_op jit(solution)/shard_map/ppermute | solution.py:32
  96.4 12.3 %collective-permute-start.9 = (bf16[96,4096]{1,0:T(8,128)(2,1)S(1)}, bf16[96,4096]{1,0:T(8,128)(2,1)S(1)}, u32[]{:S(2)}, u32[]{:S(2)}) collective-permute-start(bf16[96,4096]{1,0:T(8,128)(2,1)S(1)} %get-tuple-element.66), channel_id=1, source_target_pairs={{0,224},{4,228},{8,232},{12,236},{16,240},{20,244},{24,248},{28,25... | collective-permute-start | bytes 2359304 | tf_op jit(solution)/shard_map/ppermute | solution.py:32
  106.2 27.9 %copy-start.9 = (f32[96,4096]{1,0:T(8,128)}, f32[96,4096]{1,0:T(8,128)S(1)}, u32[]{:S(2)}) copy-start(f32[96,4096]{1,0:T(8,128)S(1)} %get-tuple-element.44) | copy-start | bytes 4718596
  108.8 12.3 %collective-permute-start.13 = (bf16[96,4096]{1,0:T(8,128)(2,1)S(1)}, bf16[96,4096]{1,0:T(8,128)(2,1)S(1)}, u32[]{:S(2)}, u32[]{:S(2)}) collective-permute-start(bf16[96,4096]{1,0:T(8,128)(2,1)S(1)} %collective-permute-done.12.refs_1_), channel_id=1, source_target_pairs={{0,32},{4,36},{8,40},{12,44},{16,48},{20,52},{24,56},{28,60},{1,33... | collective-permute-start | bytes 2359304 | tf_op jit(solution)/shard_map/ppermute | solution.py:32
  108.9 13.0 %collective-permute-start.10 = (bf16[96,4096]{1,0:T(8,128)(2,1)S(1)}, bf16[96,4096]{1,0:T(8,128)(2,1)S(1)}, u32[]{:S(2)}, u32[]{:S(2)}) collective-permute-start(bf16[96,4096]{1,0:T(8,128)(2,1)S(1)} %broadcast_select_fusion.1), channel_id=1, source_target_pairs={{0,224},{4,228},{8,232},{12,236},{16,240},{20,244},{24,248},{28,25... | collective-permute-start | bytes 2359304 | tf_op jit(solution)/shard_map/ppermute | solution.py:32
  117.6 4.3 %copy-start.13 = (f32[96,4096]{1,0:T(8,128)}, f32[96,4096]{1,0:T(8,128)S(1)}, u32[]{:S(2)}) copy-start(f32[96,4096]{1,0:T(8,128)S(1)} %get-tuple-element.43) | copy-start | bytes 4718596
  121.1 7.5 %collective-permute-start.14 = (bf16[48,4096]{1,0:T(8,128)(2,1)S(1)}, bf16[48,4096]{1,0:T(8,128)(2,1)S(1)}, u32[]{:S(2)}, u32[]{:S(2)}) collective-permute-start(bf16[48,4096]{1,0:T(8,128)(2,1)S(1)} %slice.52), channel_id=1, source_target_pairs={{0,32},{4,36},{8,40},{12,44},{16,48},{20,52},{24,56},{28,60},{1,33... | collective-permute-start | bytes 1179656 | tf_op jit(solution)/shard_map/ppermute | solution.py:32
  121.9 6.7 %collective-permute-start.11 = (bf16[48,4096]{1,0:T(8,128)(2,1)S(1)}, bf16[48,4096]{1,0:T(8,128)(2,1)S(1)}, u32[]{:S(2)}, u32[]{:S(2)}) collective-permute-start(bf16[48,4096]{1,0:T(8,128)(2,1)S(1)} %slice.64), channel_id=1, source_target_pairs={{0,224},{4,228},{8,232},{12,236},{16,240},{20,244},{24,248},{28,25... | collective-permute-start | bytes 1179656 | tf_op jit(solution)/shard_map/ppermute | solution.py:32
  128.6 5.6 %copy-start.5 = (f32[96,4096]{1,0:T(8,128)}, f32[96,4096]{1,0:T(8,128)S(1)}, u32[]{:S(2)}) copy-start(f32[96,4096]{1,0:T(8,128)S(1)} %get-tuple-element.40) | copy-start | bytes 4718596
  135.6 12.4 %collective-permute-start.15 = (bf16[96,4096]{1,0:T(8,128)(2,1)}, bf16[96,4096]{1,0:T(8,128)(2,1)}, u32[]{:S(2)}, u32[]{:S(2)}) collective-permute-start(bf16[96,4096]{1,0:T(8,128)(2,1)} %get-tuple-element.59), channel_id=1, source_target_pairs={{0,32},{4,36},{8,40},{12,44},{16,48},{20,52},{24,56},{28,60},{1,33... | collective-permute-start | bytes 2359304 | tf_op jit(solution)/shard_map/ppermute | solution.py:32
  137.7 12.0 %copy-start.14 = (f32[96,4096]{1,0:T(8,128)S(1)}, f32[96,4096]{1,0:T(8,128)}, u32[]{:S(2)}) copy-start(f32[96,4096]{1,0:T(8,128)} %copy-done.13) | copy-start | bytes 4718596
  137.7 12.0 %collective-permute-start.17 = (bf16[96,4096]{1,0:T(8,128)(2,1)}, bf16[96,4096]{1,0:T(8,128)(2,1)S(1)}, u32[]{:S(2)}, u32[]{:S(2)}) collective-permute-start(bf16[96,4096]{1,0:T(8,128)(2,1)} %get-tuple-element.60), channel_id=1, source_target_pairs={{0,224},{4,228},{8,232},{12,236},{16,240},{20,244},{24,248},{28,25... | collective-permute-start | bytes 2359304 | tf_op jit(solution)/shard_map/ppermute | solution.py:32
  149.4 12.7 %copy-start.6 = (f32[96,4096]{1,0:T(8,128)S(1)}, f32[96,4096]{1,0:T(8,128)}, u32[]{:S(2)}) copy-start(f32[96,4096]{1,0:T(8,128)} %copy-done.5) | copy-start | bytes 4718596
  149.4 12.6 %collective-permute-start.16 = (bf16[96,4096]{1,0:T(8,128)(2,1)S(1)}, bf16[96,4096]{1,0:T(8,128)(2,1)S(1)}, u32[]{:S(2)}, u32[]{:S(2)}) collective-permute-start(bf16[96,4096]{1,0:T(8,128)(2,1)S(1)} %add_convert_fusion.3), channel_id=1, source_target_pairs={{0,32},{4,36},{8,40},{12,44},{16,48},{20,52},{24,56},{28,60},{1,33... | collective-permute-start | bytes 2359304 | tf_op jit(solution)/shard_map/ppermute | solution.py:32
  149.9 12.5 %collective-permute-start.18 = (bf16[96,4096]{1,0:T(8,128)(2,1)S(1)}, bf16[96,4096]{1,0:T(8,128)(2,1)S(1)}, u32[]{:S(2)}, u32[]{:S(2)}) collective-permute-start(bf16[96,4096]{1,0:T(8,128)(2,1)S(1)} %add_convert_fusion.2), channel_id=1, source_target_pairs={{0,224},{4,228},{8,232},{12,236},{16,240},{20,244},{24,248},{28,25... | collective-permute-start | bytes 2359304 | tf_op jit(solution)/shard_map/ppermute | solution.py:32
  162.3 12.4 %collective-permute-start.22 = (bf16[96,4096]{1,0:T(8,128)(2,1)S(1)}, bf16[96,4096]{1,0:T(8,128)(2,1)S(1)}, u32[]{:S(2)}, u32[]{:S(2)}) collective-permute-start(bf16[96,4096]{1,0:T(8,128)(2,1)S(1)} %select_convert_fusion), channel_id=1, source_target_pairs={{0,32},{4,36},{8,40},{12,44},{16,48},{20,52},{24,56},{28,60},{1,33... | collective-permute-start | bytes 2359304 | tf_op jit(solution)/shard_map/ppermute | solution.py:32
  162.4 8.1 %copy-start.10 = (f32[96,4096]{1,0:T(8,128)S(1)}, f32[96,4096]{1,0:T(8,128)}, u32[]{:S(2)}) copy-start(f32[96,4096]{1,0:T(8,128)} %copy-done.9) | copy-start | bytes 4718596
  162.8 12.2 %collective-permute-start.21 = (bf16[24,4096]{1,0:T(8,128)(2,1)S(1)}, bf16[24,4096]{1,0:T(8,128)(2,1)S(1)}, u32[]{:S(2)}, u32[]{:S(2)}) collective-permute-start(bf16[24,4096]{1,0:T(8,128)(2,1)S(1)} %get-tuple-element.63), channel_id=1, source_target_pairs={{2,226},{6,230},{10,234},{14,238},{18,242},{22,246},{26,250},{30,2... | collective-permute-start | bytes 589832 | tf_op jit(solution)/shard_map/ppermute | solution.py:32
  166.1 12.4 %collective-permute-start.20 = (bf16[24,4096]{1,0:T(8,128)(2,1)S(1)}, bf16[24,4096]{1,0:T(8,128)(2,1)S(1)}, u32[]{:S(2)}, u32[]{:S(2)}) collective-permute-start(bf16[24,4096]{1,0:T(8,128)(2,1)S(1)} %get-tuple-element.64), channel_id=1, source_target_pairs={{2,66},{6,70},{10,74},{14,78},{18,82},{22,86},{26,90},{30,94},{3,6... | collective-permute-start | bytes 589832 | tf_op jit(solution)/shard_map/ppermute | solution.py:32
  168.4 6.3 %copy-start.12 = (f32[96,4096]{1,0:T(8,128)S(1)}, f32[96,4096]{1,0:T(8,128)}, u32[]{:S(2)}) copy-start(f32[96,4096]{1,0:T(8,128)} %copy-done.11) | copy-start | bytes 4718596
  168.4 13.4 %collective-permute-start.19 = (bf16[24,4096]{1,0:T(8,128)(2,1)S(1)}, bf16[24,4096]{1,0:T(8,128)(2,1)S(1)}, u32[]{:S(2)}, u32[]{:S(2)}) collective-permute-start(bf16[24,4096]{1,0:T(8,128)(2,1)S(1)} %get-tuple-element.65), channel_id=1, source_target_pairs={{2,34},{6,38},{10,42},{14,46},{18,50},{22,54},{26,58},{30,62},{3,3... | collective-permute-start | bytes 589832 | tf_op jit(solution)/shard_map/ppermute | solution.py:32
  170.6 13.2 %copy-start.16 = (bf16[3,8,16,256]{3,1,2,0:T(8,128)(2,1)S(1)}, bf16[3,8,16,256]{3,1,2,0:T(8,128)(2,1)}, u32[]{:S(2)}) copy-start(bf16[3,8,16,256]{3,1,2,0:T(8,128)(2,1)} %copy-done.15) | copy-start | bytes 589828
  170.6 13.2 %copy-start.20 = (bf16[4096,8]{0,1:T(8,128)(2,1)S(1)}, bf16[4096,8]{0,1:T(8,128)(2,1)}, u32[]{:S(2)}) copy-start(bf16[4096,8]{0,1:T(8,128)(2,1)} %param.14) | copy-start | bytes 196612
  170.6 19.5 %copy-start.8 = (f32[96,4096]{1,0:T(8,128)S(1)}, f32[96,4096]{1,0:T(8,128)}, u32[]{:S(2)}) copy-start(f32[96,4096]{1,0:T(8,128)} %copy-done.7) | copy-start | bytes 4718596
  170.6 19.5 %collective-permute-start.25 = (bf16[96,4096]{1,0:T(8,128)(2,1)S(1)}, bf16[96,4096]{1,0:T(8,128)(2,1)S(1)}, u32[]{:S(2)}, u32[]{:S(2)}) collective-permute-start(bf16[96,4096]{1,0:T(8,128)(2,1)S(1)} %add_convert_fusion), channel_id=1, source_target_pairs={{0,224},{4,228},{8,232},{12,236},{16,240},{20,244},{24,248},{28,25... | collective-permute-start | bytes 2359304 | tf_op jit(solution)/shard_map/ppermute | solution.py:32
  174.9 15.2 %collective-permute-start.24 = (bf16[96,4096]{1,0:T(8,128)(2,1)S(1)}, bf16[96,4096]{1,0:T(8,128)(2,1)S(1)}, u32[]{:S(2)}, u32[]{:S(2)}) collective-permute-start(bf16[96,4096]{1,0:T(8,128)(2,1)S(1)} %add_convert_fusion.1), channel_id=1, source_target_pairs={{0,32},{4,36},{8,40},{12,44},{16,48},{20,52},{24,56},{28,60},{1,33... | collective-permute-start | bytes 2359304 | tf_op jit(solution)/shard_map/ppermute | solution.py:32
  181.8 8.3 %collective-permute-start.23 = (bf16[24,4096]{1,0:T(8,128)(2,1)S(1)}, bf16[24,4096]{1,0:T(8,128)(2,1)S(1)}, u32[]{:S(2)}, u32[]{:S(2)}) collective-permute-start(bf16[24,4096]{1,0:T(8,128)(2,1)S(1)} %fusion.17), channel_id=1, source_target_pairs={{2,194},{6,198},{10,202},{14,206},{18,210},{22,214},{26,218},{30,2... | collective-permute-start | bytes 589832 | tf_op jit(solution)/shard_map/ppermute | solution.py:32
  190.5 6.5 %collective-permute-start.26 = (bf16[24,4096]{1,0:T(8,128)(2,1)S(1)}, bf16[24,4096]{1,0:T(8,128)(2,1)S(1)}, u32[]{:S(2)}, u32[]{:S(2)}) collective-permute-start(bf16[24,4096]{1,0:T(8,128)(2,1)S(1)} %get-tuple-element.61), channel_id=1, source_target_pairs={{0,16},{4,20},{8,24},{12,28},{16,1},{20,5},{24,9},{28,13},{1,17},{... | collective-permute-start | bytes 589832 | tf_op jit(solution)/shard_map/ppermute | solution.py:32
  190.6 6.4 %collective-permute-start.27 = (bf16[24,4096]{1,0:T(8,128)(2,1)S(1)}, bf16[24,4096]{1,0:T(8,128)(2,1)S(1)}, u32[]{:S(2)}, u32[]{:S(2)}) collective-permute-start(bf16[24,4096]{1,0:T(8,128)(2,1)S(1)} %get-tuple-element.62), channel_id=1, source_target_pairs={{0,17},{4,21},{8,25},{12,29},{16,0},{20,4},{24,8},{28,12},{1,16},{... | collective-permute-start | bytes 589832 | tf_op jit(solution)/shard_map/ppermute | solution.py:32
  193.3 24.9 %copy-start.18 = (bf16[128,256]{1,0:T(8,128)(2,1)S(1)}, bf16[128,256]{1,0:T(8,128)(2,1)}, u32[]{:S(2)}) copy-start(bf16[128,256]{1,0:T(8,128)(2,1)} %param.12) | copy-start | bytes 196612
  193.3 8.4 %collective-permute-start.28 = (bf16[24,4096]{1,0:T(8,128)(2,1)S(1)}, bf16[24,4096]{1,0:T(8,128)(2,1)S(1)}, u32[]{:S(2)}, u32[]{:S(2)}) collective-permute-start(bf16[24,4096]{1,0:T(8,128)(2,1)S(1)} %fusion.11), channel_id=1, source_target_pairs={{0,1},{4,5},{8,9},{12,13},{16,17},{20,21},{24,25},{28,29},{1,0},{5... | collective-permute-start | bytes 589832 | tf_op jit(solution)/shard_map/ppermute | solution.py:32
  (4 other events, 5.8 us)

commit v2 on v1

--- a/solution.py
+++ b/solution.py
@@ -240,18 +240,18 @@
     both = lax.optimization_barrier((plus_2, minus_2))
     rest = sum_last + f32(both[0]) + f32(both[1])
     rest = [rest[k * n : (k + 1) * n] for k in range(4)]
-    from_1, from_2 = hop(b16(rest[1]), None, (1, 0)), hop(b16(rest[3]), None, (2, 0))
+    from_1, from_2 = hop(b16(rest[1]), None, (1, 0)), hop(b16(rest[3]), None, (-2, 0))
     from_above = hop(b16(rest[2]), None, (-1, 0))
     from_1, from_2, from_above, _ = lax.optimization_barrier((from_1, from_2, from_above, plus_3))
     plus_4 = hop(b16(sums[1][0] + f32(plus_3)), (1, 0), (0, 1))
-    last_down = hop(b16(rest[0] + f32(from_above)), None, (-2, 0))
+    last_down = hop(b16(rest[0] + f32(from_above) + f32(from_2)), None, (-2, 0))
     last_down, plus_4 = lax.optimization_barrier((last_down, plus_4))
     total = sum_own + f32(plus_4) + f32(pick(minus_3, minus_1))
     chunk = [total[k * n : (k + 1) * n] for k in range(4)]
     result = chunk[0] + f32(last_down)
     result = result + f32(hop(b16(chunk[1]), (0, 1), (1, 0)))
     result = result + f32(hop(b16(chunk[2]), (0, -1), (-1, 0)))
-    result = result + f32(hop(b16(chunk[3] + f32(from_1) + f32(from_2)), (0, 2), (2, 0)))
+    result = result + f32(hop(b16(chunk[3] + f32(from_1)), (0, 2), (2, 0)))
 
     back = (result * weight[:, None]).astype(jnp.bfloat16).reshape(half_cap, n_exp * n_ffn, span)
     returned = lax.all_to_all(

time: 220 us -> 214 us (0.973)
  waiting for transfers between devices: 82.4 us -> 75.5 us
  starting transfers between devices: 67.5 us -> 70.4 us
    ppermute x29, waiting for transfers between devices: 50.7 us -> 43.8 us  [hop(): return lax.ppermute(value, ALL, pairs)]
    ppermute x29, starting transfers between devices: 46.5 us -> 49.4 us  [hop(): return lax.ppermute(value, ALL, pairs)]
where the time goes in v2:
time: 214 us; the launch traced here: 213 us
  waiting for transfers between devices  75.5 us (35%)
  starting transfers between devices  70.4 us (33%)
  Pallas kernels  28.5 us (13%)
  blocking collectives  14.7 us (7%)
  local copies, waits for them, and re-layouts  12.3 us (6%)
  other arithmetic  7.33 us (3%)
  matrix products  3.76 us (2%)
    ppermute x29, starting transfers between devices, hop(): return lax.ppermute(value, ALL, pairs)  49.4 us
    ppermute x29, waiting for transfers between devices, hop(): return lax.ppermute(value, ALL, pairs)  43.8 us
    pallas_call x5, Pallas kernels, expert(): pl.pallas_call(functools.partial(expert_kernel, tuple(places), tuple(outs...  28.5 us
    all_to_all x1, waiting for transfers between devices, shards(): lax.all_to_all(jnp.broadcast_to(pair[None], (n_seq,) + pair.shape), 'seq'...  23.5 us
    all_to_all x1, blocking collectives, shards(): lax.all_to_all(back, ('expert', 'ffn'), split_axis=1, concat_axis=0, tile...  14.7 us
    all_to_all x1, starting transfers between devices, shards(): lax.all_to_all(send, ('expert', 'ffn'), split_axis=0, concat_axis=2, tile...  11 us
    all_to_all x1, starting transfers between devices, shards(): lax.all_to_all(jnp.broadcast_to(pair[None], (n_seq,) + pair.shape), 'seq'...  10 us
    unnamed x50, local copies, waits for them, and re-layouts  8.44 us
  transfers between devices with their start and end apart: 31, of which 13 were waited for; matrix products, arithmetic and copies ran while one was open for 3% of the time, Pallas kernels for 11%

profile of v2, /device:TPU:1, one launch (start us, length us, event | category | flops | bytes accessed | tf_op | source)
XLA Modules:
  0.0 213.4 jit_solution(3017134630002182274)
XLA Ops:
  0.8 1.1 broadcast_in_dim.52
  1.9 10.0 %all-to-all-start = ((bf16[16,128,256]{2,1,0:T(8,128)(2,1)}), bf16[16,128,256]{2,1,0:T(8,128)(2,1)S(1)}, u32[]{:S(2)}, u32[]{:S(2)}) async-start(bf16[16,128,256]{2,1,0:T(8,128)(2,1)} %broadcast_in_dim.52), calls=%async_computation | async-start | bytes 2097152 | tf_op jit(solution)/shard_map/all_to_all | solution.py:154
  13.8 23.5 %all-to-all-done = bf16[16,128,256]{2,1,0:T(8,128)(2,1)S(1)} async-done(((bf16[16,128,256]{2,1,0:T(8,128)(2,1)}), bf16[16,128,256]{2,1,0:T(8,128)(2,1)S(1)}, u32[]{:S(2)}, u32[]{:S(2)}) %all-to-all-start) | async-done | bytes 1048608 | tf_op jit(solution)/shard_map/all_to_all | solution.py:154
  38.2 1.3 fusion.5
  39.7 0.9 convolution_convert_fusion
  40.5 11.0 %all-to-all-start.1 = ((bf16[16,24,1,256]{3,1,2,0:T(8,128)(2,1)}), bf16[16,24,1,256]{3,1,2,0:T(8,128)(2,1)S(1)}, u32[]{:S(2)}, u32[]{:S(2)}) async-start(bf16[16,24,1,256]{3,1,2,0:T(8,128)(2,1)} %bitcast.10), calls=%async_computation.1 | async-start | bytes 393216 | tf_op jit(solution)/shard_map/all_to_all | solution.py:174
  51.5 8.3 %all-to-all-done.1 = bf16[16,24,1,256]{3,1,2,0:T(8,128)(2,1)S(1)} async-done(((bf16[16,24,1,256]{3,1,2,0:T(8,128)(2,1)}), bf16[16,24,1,256]{3,1,2,0:T(8,128)(2,1)S(1)}, u32[]{:S(2)}, u32[]{:S(2)}) %all-to-all-start.1) | async-done | bytes 196640 | tf_op jit(solution)/shard_map/all_to_all | solution.py:174
  59.8 2.0 collective-permute-start.5
  61.9 3.5 %collective-permute-start.2 = (bf16[24,4096]{1,0:T(8,128)(2,1)S(1)}, bf16[24,4096]{1,0:T(8,128)(2,1)S(1)}, u32[]{:S(2)}, u32[]{:S(2)}) collective-permute-start(bf16[24,4096]{1,0:T(8,128)(2,1)S(1)} %bitcast.88), channel_id=1, source_target_pairs={{0,1},{4,5},{8,9},{12,13},{16,17},{20,21},{24,25},{28,29},{1,0},{5... | collective-permute-start | bytes 589832 | tf_op jit(solution)/shard_map/ppermute | solution.py:32
  65.4 2.7 %collective-permute-start = (bf16[24,4096]{1,0:T(8,128)(2,1)S(1)}, bf16[24,4096]{1,0:T(8,128)(2,1)S(1)}, u32[]{:S(2)}, u32[]{:S(2)}) collective-permute-start(bf16[24,4096]{1,0:T(8,128)(2,1)S(1)} %bitcast.90), channel_id=1, source_target_pairs={{0,17},{4,21},{8,25},{12,29},{16,0},{20,4},{24,8},{28,12},{1,16},{... | collective-permute-start | bytes 589832 | tf_op jit(solution)/shard_map/ppermute | solution.py:32
  68.1 3.6 %collective-permute-done = bf16[24,4096]{1,0:T(8,128)(2,1)S(1)} collective-permute-done((bf16[24,4096]{1,0:T(8,128)(2,1)S(1)}, bf16[24,4096]{1,0:T(8,128)(2,1)S(1)}, u32[]{:S(2)}, u32[]{:S(2)}) %collective-permute-start) | collective-permute-done | bytes 196640 | tf_op jit(solution)/shard_map/ppermute | solution.py:32
  71.9 1.5 collective-permute-start.3
  73.3 5.1 %collective-permute-start.8 = (bf16[24,4096]{1,0:T(8,128)(2,1)S(1)}, bf16[24,4096]{1,0:T(8,128)(2,1)S(1)}, u32[]{:S(2)}, u32[]{:S(2)}) collective-permute-start(bf16[24,4096]{1,0:T(8,128)(2,1)S(1)} %collective-permute-done.2), channel_id=1, source_target_pairs={{2,194},{6,198},{10,202},{14,206},{18,210},{22,214},{26,218},{30,2... | collective-permute-start | bytes 589832 | tf_op jit(solution)/shard_map/ppermute | solution.py:32
  78.5 2.1 collective-permute-start.6
  80.6 3.2 %collective-permute-start.7 = (bf16[24,4096]{1,0:T(8,128)(2,1)S(1)}, bf16[24,4096]{1,0:T(8,128)(2,1)S(1)}, u32[]{:S(2)}, u32[]{:S(2)}) collective-permute-start(bf16[24,4096]{1,0:T(8,128)(2,1)S(1)} %collective-permute-done.5), channel_id=1, source_target_pairs={{2,34},{6,38},{10,42},{14,46},{18,50},{22,54},{26,58},{30,62},{3,3... | collective-permute-start | bytes 589832 | tf_op jit(solution)/shard_map/ppermute | solution.py:32
  83.8 2.0 copy-done.1
  85.8 2.0 copy-done.3
  87.9 2.0 copy-done.4
  89.9 5.3 %shard_map.91 = f32[96,4096]{1,0:T(8,128)S(1)} custom-call(bf16[96,4096]{1,0:T(8,128)(2,1)S(1)} %constant_dynamic-update-slice_fusion.refs_0_, bf16[448,4096]{1,0:T(8,128)(2,1)S(1)} %bitcast.69, bf16[448,4096]{1,0:T(8,128)(2,1)S(1)} %bitcast.74, bf16[448,4096]{1,0:T(8,128)(2,1)S(1)} %bitcast.79), custom_call_target="tpu_custom_call" | custom-call | flops 1056964608 | bytes 13369344 | tf_op jit(solution)/shard_map/pallas_call | solution.py:98
  95.5 0.9 copy-done.7
  96.4 2.7 %collective-permute-start.9 = (bf16[96,4096]{1,0:T(8,128)(2,1)S(1)}, bf16[96,4096]{1,0:T(8,128)(2,1)S(1)}, u32[]{:S(2)}, u32[]{:S(2)}) collective-permute-start(bf16[96,4096]{1,0:T(8,128)(2,1)S(1)} %get-tuple-element.66), channel_id=1, source_target_pairs={{0,224},{4,228},{8,232},{12,236},{16,240},{20,244},{24,248},{28,25... | collective-permute-start | bytes 2359304 | tf_op jit(solution)/shard_map/ppermute | solution.py:32
  99.1 6.0 %shard_map.92 = (f32[96,4096]{1,0:T(8,128)S(1)}, f32[96,4096]{1,0:T(8,128)S(1)}) custom-call(bf16[96,4096]{1,0:T(8,128)(2,1)S(1)} %collective-permute-done.4.refs_0_, bf16[96,4096]{1,0:T(8,128)(2,1)S(1)} %collective-permute-done.3.refs_1_, bf16[448,4096]{1,0:T(8,128)(2,1)S(1)} %bitcast.70, bf16[448,4096]{1,0:T(8,128)(2,1)S(1)} %bitcast.75, ...), custom_call_target="tpu_custom_call" | custom-call | flops 2113929216 | bytes 15728640 | tf_op jit(solution)/shard_map/pallas_call | solution.py:98
  105.1 1.1 copy-done.11
  106.2 2.5 %collective-permute-done.12.refs_1_ = bf16[96,4096]{1,0:T(8,128)(2,1)S(1)} collective-permute-done((bf16[96,4096]{1,0:T(8,128)(2,1)S(1)}, bf16[96,4096]{1,0:T(8,128)(2,1)S(1)}, u32[]{:S(2)}, u32[]{:S(2)}) %collective-permute-start.12) | collective-permute-done | bytes 786464 | tf_op jit(solution)/shard_map/ppermute | solution.py:32
  108.9 2.8 %collective-permute-start.10 = (bf16[96,4096]{1,0:T(8,128)(2,1)S(1)}, bf16[96,4096]{1,0:T(8,128)(2,1)S(1)}, u32[]{:S(2)}, u32[]{:S(2)}) collective-permute-start(bf16[96,4096]{1,0:T(8,128)(2,1)S(1)} %broadcast_select_fusion.1), channel_id=1, source_target_pairs={{0,224},{4,228},{8,232},{12,236},{16,240},{20,244},{24,248},{28,25... | collective-permute-start | bytes 2359304 | tf_op jit(solution)/shard_map/ppermute | solution.py:32
  111.6 6.0 %shard_map.93 = (f32[96,4096]{1,0:T(8,128)S(1)}, f32[96,4096]{1,0:T(8,128)S(1)}) custom-call(bf16[96,4096]{1,0:T(8,128)(2,1)S(1)} %collective-permute-done.9.refs_0_, bf16[96,4096]{1,0:T(8,128)(2,1)S(1)} %collective-permute-done.12.refs_1_, bf16[448,4096]{1,0:T(8,128)(2,1)S(1)} %bitcast.71, bf16[448,4096]{1,0:T(8,128)(2,1)S(1)} %bitcast.76, ...), custom_call_target="tpu_custom_call" | custom-call | flops 2113929216 | bytes 15728640 | tf_op jit(solution)/shard_map/pallas_call | solution.py:98
  117.6 3.5 %collective-permute-done.13.refs_1_ = bf16[96,4096]{1,0:T(8,128)(2,1)S(1)} collective-permute-done((bf16[96,4096]{1,0:T(8,128)(2,1)S(1)}, bf16[96,4096]{1,0:T(8,128)(2,1)S(1)}, u32[]{:S(2)}, u32[]{:S(2)}) %collective-permute-start.13) | collective-permute-done | bytes 786464 | tf_op jit(solution)/shard_map/ppermute | solution.py:32
  122.6 6.0 %shard_map.94 = (f32[96,4096]{1,0:T(8,128)S(1)}, f32[96,4096]{1,0:T(8,128)S(1)}) custom-call(bf16[96,4096]{1,0:T(8,128)(2,1)S(1)} %collective-permute-done.10.refs_0_, bf16[96,4096]{1,0:T(8,128)(2,1)S(1)} %collective-permute-done.13.refs_1_, bf16[448,4096]{1,0:T(8,128)(2,1)S(1)} %bitcast.72, bf16[448,4096]{1,0:T(8,128)(2,1)S(1)} %bitcast.77, ...), custom_call_target="tpu_custom_call" | custom-call | flops 2113929216 | bytes 15728640 | tf_op jit(solution)/shard_map/pallas_call | solution.py:98
  128.8 5.3 %shard_map.95 = f32[96,4096]{1,0:T(8,128)S(1)} custom-call(bf16[96,4096]{1,0:T(8,128)(2,1)S(1)} %maximum_select_fusion.refs_0_, bf16[448,4096]{1,0:T(8,128)(2,1)S(1)} %bitcast.73, bf16[448,4096]{1,0:T(8,128)(2,1)S(1)} %bitcast.78, bf16[448,4096]{1,0:T(8,128)(2,1)S(1)} %bitcast.83), custom_call_target="tpu_custom_call" | custom-call | flops 1056964608 | bytes 13369344 | tf_op jit(solution)/shard_map/pallas_call | solution.py:98
  134.2 1.5 select_convert_fusion.2
  136.4 1.0 mul.60
  137.7 2.8 %collective-permute-start.17 = (bf16[96,4096]{1,0:T(8,128)(2,1)}, bf16[96,4096]{1,0:T(8,128)(2,1)S(1)}, u32[]{:S(2)}, u32[]{:S(2)}) collective-permute-start(bf16[96,4096]{1,0:T(8,128)(2,1)} %get-tuple-element.60), channel_id=1, source_target_pairs={{0,224},{4,228},{8,232},{12,236},{16,240},{20,244},{24,248},{28,25... | collective-permute-start | bytes 2359304 | tf_op jit(solution)/shard_map/ppermute | solution.py:32
  140.4 7.6 %collective-permute-done.15 = bf16[96,4096]{1,0:T(8,128)(2,1)} collective-permute-done((bf16[96,4096]{1,0:T(8,128)(2,1)}, bf16[96,4096]{1,0:T(8,128)(2,1)}, u32[]{:S(2)}, u32[]{:S(2)}) %collective-permute-start.15) | collective-permute-done | bytes 786464 | tf_op jit(solution)/shard_map/ppermute | solution.py:32
  148.0 1.3 add_convert_fusion.3
  149.9 3.1 %collective-permute-start.18 = (bf16[96,4096]{1,0:T(8,128)(2,1)S(1)}, bf16[96,4096]{1,0:T(8,128)(2,1)S(1)}, u32[]{:S(2)}, u32[]{:S(2)}) collective-permute-start(bf16[96,4096]{1,0:T(8,128)(2,1)S(1)} %add_convert_fusion.2), channel_id=1, source_target_pairs={{0,224},{4,228},{8,232},{12,236},{16,240},{20,244},{24,248},{28,25... | collective-permute-start | bytes 2359304 | tf_op jit(solution)/shard_map/ppermute | solution.py:32
  153.0 9.0 %collective-permute-done.16 = bf16[96,4096]{1,0:T(8,128)(2,1)S(1)} collective-permute-done((bf16[96,4096]{1,0:T(8,128)(2,1)S(1)}, bf16[96,4096]{1,0:T(8,128)(2,1)S(1)}, u32[]{:S(2)}, u32[]{:S(2)}) %collective-permute-start.16) | collective-permute-done | bytes 786464 | tf_op jit(solution)/shard_map/ppermute | solution.py:32
  162.8 3.3 %collective-permute-start.21 = (bf16[24,4096]{1,0:T(8,128)(2,1)S(1)}, bf16[24,4096]{1,0:T(8,128)(2,1)S(1)}, u32[]{:S(2)}, u32[]{:S(2)}) collective-permute-start(bf16[24,4096]{1,0:T(8,128)(2,1)S(1)} %get-tuple-element.63), channel_id=1, source_target_pairs={{2,226},{6,230},{10,234},{14,238},{18,242},{22,246},{26,250},{30,2... | collective-permute-start | bytes 589832 | tf_op jit(solution)/shard_map/ppermute | solution.py:32
  166.1 1.9 collective-permute-start.20
  168.0 3.2 %collective-permute-start.19 = (bf16[24,4096]{1,0:T(8,128)(2,1)S(1)}, bf16[24,4096]{1,0:T(8,128)(2,1)S(1)}, u32[]{:S(2)}, u32[]{:S(2)}) collective-permute-start(bf16[24,4096]{1,0:T(8,128)(2,1)S(1)} %get-tuple-element.65), channel_id=1, source_target_pairs={{2,34},{6,38},{10,42},{14,46},{18,50},{22,54},{26,58},{30,62},{3,3... | collective-permute-start | bytes 589832 | tf_op jit(solution)/shard_map/ppermute | solution.py:32
  172.3 2.4 %collective-permute-done.22 = bf16[96,4096]{1,0:T(8,128)(2,1)S(1)} collective-permute-done((bf16[96,4096]{1,0:T(8,128)(2,1)S(1)}, bf16[96,4096]{1,0:T(8,128)(2,1)S(1)}, u32[]{:S(2)}, u32[]{:S(2)}) %collective-permute-start.22) | collective-permute-done | bytes 786464 | tf_op jit(solution)/shard_map/ppermute | solution.py:32
  175.0 2.7 %collective-permute-done.20 = bf16[24,4096]{1,0:T(8,128)(2,1)S(1)} collective-permute-done((bf16[24,4096]{1,0:T(8,128)(2,1)S(1)}, bf16[24,4096]{1,0:T(8,128)(2,1)S(1)}, u32[]{:S(2)}, u32[]{:S(2)}) %collective-permute-start.20) | collective-permute-done | bytes 196640 | tf_op jit(solution)/shard_map/ppermute | solution.py:32
  177.7 1.9 collective-permute-start.23
  179.9 7.1 %collective-permute-done.23 = bf16[24,4096]{1,0:T(8,128)(2,1)S(1)} collective-permute-done((bf16[24,4096]{1,0:T(8,128)(2,1)S(1)}, bf16[24,4096]{1,0:T(8,128)(2,1)S(1)}, u32[]{:S(2)}, u32[]{:S(2)}) %collective-permute-start.23) | collective-permute-done | bytes 196640 | tf_op jit(solution)/shard_map/ppermute | solution.py:32
  187.8 2.2 %collective-permute-start.28 = (bf16[24,4096]{1,0:T(8,128)(2,1)S(1)}, bf16[24,4096]{1,0:T(8,128)(2,1)S(1)}, u32[]{:S(2)}, u32[]{:S(2)}) collective-permute-start(bf16[24,4096]{1,0:T(8,128)(2,1)S(1)} %fusion.10), channel_id=1, source_target_pairs={{0,1},{4,5},{8,9},{12,13},{16,17},{20,21},{24,25},{28,29},{1,0},{5... | collective-permute-start | bytes 589832 | tf_op jit(solution)/shard_map/ppermute | solution.py:32
  190.3 2.4 %collective-permute-start.27 = (bf16[24,4096]{1,0:T(8,128)(2,1)S(1)}, bf16[24,4096]{1,0:T(8,128)(2,1)S(1)}, u32[]{:S(2)}, u32[]{:S(2)}) collective-permute-start(bf16[24,4096]{1,0:T(8,128)(2,1)S(1)} %get-tuple-element.62), channel_id=1, source_target_pairs={{0,17},{4,21},{8,25},{12,29},{16,0},{20,4},{24,8},{28,12},{1,16},{... | collective-permute-start | bytes 589832 | tf_op jit(solution)/shard_map/ppermute | solution.py:32
  192.7 4.2 %collective-permute-done.28 = bf16[24,4096]{1,0:T(8,128)(2,1)S(1)} collective-permute-done((bf16[24,4096]{1,0:T(8,128)(2,1)S(1)}, bf16[24,4096]{1,0:T(8,128)(2,1)S(1)}, u32[]{:S(2)}, u32[]{:S(2)}) %collective-permute-start.28) | collective-permute-done | bytes 196640 | tf_op jit(solution)/shard_map/ppermute | solution.py:32
  197.9 14.7 %all_to_all.35 = bf16[24,16,256]{2,0,1:T(8,128)(2,1)S(1)} all-to-all(bf16[24,16,256]{2,0,1:T(8,128)(2,1)S(1)} %bitcast.94), channel_id=1, replica_groups=mesh['seq'=16,'expert'=8,'ffn'=2] {'expert','ffn'}, dimensions={1} | all-to-all | bytes 393216 | tf_op jit(solution)/shard_map/all_to_all | solution.py:257
  212.6 0.9 fusion.6
  (123 shorter events, 11.6 us)
Async XLA Ops:
  0.0 37.3 %copy-start = (bf16[128,256]{1,0:T(8,128)(2,1)S(1)}, bf16[128,256]{1,0:T(8,128)(2,1)}, u32[]{:S(2)}) copy-start(bf16[128,256]{1,0:T(8,128)(2,1)} %param.9) | copy-start | bytes 196612
  0.8 11.2 %copy-start.19 = (s32[128,2]{0,1:T(2,128)S(1)}, s32[128,2]{0,1:T(2,128)}, u32[]{:S(2)}) copy-start(s32[128,2]{0,1:T(2,128)} %param.13) | copy-start | bytes 3076
  1.9 35.4 %all-to-all-start = ((bf16[16,128,256]{2,1,0:T(8,128)(2,1)}), bf16[16,128,256]{2,1,0:T(8,128)(2,1)S(1)}, u32[]{:S(2)}, u32[]{:S(2)}) async-start(bf16[16,128,256]{2,1,0:T(8,128)(2,1)} %broadcast_in_dim.52), calls=%async_computation | async-start | bytes 2097152 | tf_op jit(solution)/shard_map/all_to_all | solution.py:154
  40.5 19.2 %all-to-all-start.1 = ((bf16[16,24,1,256]{3,1,2,0:T(8,128)(2,1)}), bf16[16,24,1,256]{3,1,2,0:T(8,128)(2,1)S(1)}, u32[]{:S(2)}, u32[]{:S(2)}) async-start(bf16[16,24,1,256]{3,1,2,0:T(8,128)(2,1)} %bitcast.10), calls=%async_computation.1 | async-start | bytes 393216 | tf_op jit(solution)/shard_map/all_to_all | solution.py:174
  59.8 35.4 %copy-start.15 = (bf16[3,8,16,256]{3,1,2,0:T(8,128)(2,1)}, bf16[3,8,16,256]{3,1,2,0:T(8,128)(2,1)S(1)}, u32[]{:S(2)}) copy-start(bf16[3,8,16,256]{3,1,2,0:T(8,128)(2,1)S(1)} %copy.68) | copy-start | bytes 589828
  59.8 20.7 %collective-permute-start.5 = (bf16[24,4096]{1,0:T(8,128)(2,1)S(1)}, bf16[24,4096]{1,0:T(8,128)(2,1)S(1)}, u32[]{:S(2)}, u32[]{:S(2)}) collective-permute-start(bf16[24,4096]{1,0:T(8,128)(2,1)S(1)} %bitcast.87), channel_id=1, source_target_pairs={{2,66},{6,70},{10,74},{14,78},{18,82},{22,86},{26,90},{30,94},{3,6... | collective-permute-start | bytes 589832 | tf_op jit(solution)/shard_map/ppermute | solution.py:32
  61.9 9.9 %collective-permute-start.2 = (bf16[24,4096]{1,0:T(8,128)(2,1)S(1)}, bf16[24,4096]{1,0:T(8,128)(2,1)S(1)}, u32[]{:S(2)}, u32[]{:S(2)}) collective-permute-start(bf16[24,4096]{1,0:T(8,128)(2,1)S(1)} %bitcast.88), channel_id=1, source_target_pairs={{0,1},{4,5},{8,9},{12,13},{16,17},{20,21},{24,25},{28,29},{1,0},{5... | collective-permute-start | bytes 589832 | tf_op jit(solution)/shard_map/ppermute | solution.py:32
  65.4 6.3 %collective-permute-start.1 = (bf16[24,4096]{1,0:T(8,128)(2,1)S(1)}, bf16[24,4096]{1,0:T(8,128)(2,1)S(1)}, u32[]{:S(2)}, u32[]{:S(2)}) collective-permute-start(bf16[24,4096]{1,0:T(8,128)(2,1)S(1)} %bitcast.89), channel_id=1, source_target_pairs={{0,16},{4,20},{8,24},{12,28},{16,1},{20,5},{24,9},{28,13},{1,17},{... | collective-permute-start | bytes 589832 | tf_op jit(solution)/shard_map/ppermute | solution.py:32
  65.4 6.3 %collective-permute-start = (bf16[24,4096]{1,0:T(8,128)(2,1)S(1)}, bf16[24,4096]{1,0:T(8,128)(2,1)S(1)}, u32[]{:S(2)}, u32[]{:S(2)}) collective-permute-start(bf16[24,4096]{1,0:T(8,128)(2,1)S(1)} %bitcast.90), channel_id=1, source_target_pairs={{0,17},{4,21},{8,25},{12,29},{16,0},{20,4},{24,8},{28,12},{1,16},{... | collective-permute-start | bytes 589832 | tf_op jit(solution)/shard_map/ppermute | solution.py:32
  71.8 23.6 %collective-permute-start.4 = (bf16[96,4096]{1,0:T(8,128)(2,1)S(1)}, bf16[96,4096]{1,0:T(8,128)(2,1)S(1)}, u32[]{:S(2)}, u32[]{:S(2)}) collective-permute-start(bf16[96,4096]{1,0:T(8,128)(2,1)S(1)} %constant_dynamic-update-slice_fusion.refs_0_), channel_id=1, source_target_pairs={{0,224},{4,228},{8,232},{12,236},{16,240},{20,244},{24,248},{28,25... | collective-permute-start | bytes 2359304 | tf_op jit(solution)/shard_map/ppermute | solution.py:32
  71.9 23.5 %collective-permute-start.3 = (bf16[96,4096]{1,0:T(8,128)(2,1)S(1)}, bf16[96,4096]{1,0:T(8,128)(2,1)S(1)}, u32[]{:S(2)}, u32[]{:S(2)}) collective-permute-start(bf16[96,4096]{1,0:T(8,128)(2,1)S(1)} %constant_dynamic-update-slice_fusion.refs_0_), channel_id=1, source_target_pairs={{0,32},{4,36},{8,40},{12,44},{16,48},{20,52},{24,56},{28,60},{1,33... | collective-permute-start | bytes 2359304 | tf_op jit(solution)/shard_map/ppermute | solution.py:32
  73.3 22.0 %collective-permute-start.8 = (bf16[24,4096]{1,0:T(8,128)(2,1)S(1)}, bf16[24,4096]{1,0:T(8,128)(2,1)S(1)}, u32[]{:S(2)}, u32[]{:S(2)}) collective-permute-start(bf16[24,4096]{1,0:T(8,128)(2,1)S(1)} %collective-permute-done.2), channel_id=1, source_target_pairs={{2,194},{6,198},{10,202},{14,206},{18,210},{22,214},{26,218},{30,2... | collective-permute-start | bytes 589832 | tf_op jit(solution)/shard_map/ppermute | solution.py:32
  78.5 16.8 %collective-permute-start.6 = (bf16[24,4096]{1,0:T(8,128)(2,1)S(1)}, bf16[24,4096]{1,0:T(8,128)(2,1)S(1)}, u32[]{:S(2)}, u32[]{:S(2)}) collective-permute-start(bf16[24,4096]{1,0:T(8,128)(2,1)S(1)} %collective-permute-done.2), channel_id=1, source_target_pairs={{2,226},{6,230},{10,234},{14,238},{18,242},{22,246},{26,250},{30,2... | collective-permute-start | bytes 589832 | tf_op jit(solution)/shard_map/ppermute | solution.py:32
  80.6 14.7 %collective-permute-start.7 = (bf16[24,4096]{1,0:T(8,128)(2,1)S(1)}, bf16[24,4096]{1,0:T(8,128)(2,1)S(1)}, u32[]{:S(2)}, u32[]{:S(2)}) collective-permute-start(bf16[24,4096]{1,0:T(8,128)(2,1)S(1)} %collective-permute-done.5), channel_id=1, source_target_pairs={{2,34},{6,38},{10,42},{14,46},{18,50},{22,54},{26,58},{30,62},{3,3... | collective-permute-start | bytes 589832 | tf_op jit(solution)/shard_map/ppermute | solution.py:32
  83.8 2.0 copy-start.1
  85.8 2.0 copy-start.3
  95.3 3.7 %copy-start.2 = (bf16[1,4096,448]{1,2,0:T(8,128)(2,1)S(1)}, bf16[1,4096,448]{1,2,0:T(8,128)(2,1)}, u32[]{:S(2)}) copy-start(bf16[1,4096,448]{1,2,0:T(8,128)(2,1)} %param.15) | copy-start | bytes 11010052
  96.4 12.3 %collective-permute-start.12 = (bf16[96,4096]{1,0:T(8,128)(2,1)S(1)}, bf16[96,4096]{1,0:T(8,128)(2,1)S(1)}, u32[]{:S(2)}, u32[]{:S(2)}) collective-permute-start(bf16[96,4096]{1,0:T(8,128)(2,1)S(1)} %get-tuple-element.67), channel_id=1, source_target_pairs={{0,32},{4,36},{8,40},{12,44},{16,48},{20,52},{24,56},{28,60},{1,33... | collective-permute-start | bytes 2359304 | tf_op jit(solution)/shard_map/ppermute | solution.py:32
  96.4 12.3 %collective-permute-start.9 = (bf16[96,4096]{1,0:T(8,128)(2,1)S(1)}, bf16[96,4096]{1,0:T(8,128)(2,1)S(1)}, u32[]{:S(2)}, u32[]{:S(2)}) collective-permute-start(bf16[96,4096]{1,0:T(8,128)(2,1)S(1)} %get-tuple-element.66), channel_id=1, source_target_pairs={{0,224},{4,228},{8,232},{12,236},{16,240},{20,244},{24,248},{28,25... | collective-permute-start | bytes 2359304 | tf_op jit(solution)/shard_map/ppermute | solution.py:32
  106.2 27.9 %copy-start.9 = (f32[96,4096]{1,0:T(8,128)}, f32[96,4096]{1,0:T(8,128)S(1)}, u32[]{:S(2)}) copy-start(f32[96,4096]{1,0:T(8,128)S(1)} %get-tuple-element.44) | copy-start | bytes 4718596
  108.8 12.3 %collective-permute-start.13 = (bf16[96,4096]{1,0:T(8,128)(2,1)S(1)}, bf16[96,4096]{1,0:T(8,128)(2,1)S(1)}, u32[]{:S(2)}, u32[]{:S(2)}) collective-permute-start(bf16[96,4096]{1,0:T(8,128)(2,1)S(1)} %collective-permute-done.12.refs_1_), channel_id=1, source_target_pairs={{0,32},{4,36},{8,40},{12,44},{16,48},{20,52},{24,56},{28,60},{1,33... | collective-permute-start | bytes 2359304 | tf_op jit(solution)/shard_map/ppermute | solution.py:32
  108.9 13.0 %collective-permute-start.10 = (bf16[96,4096]{1,0:T(8,128)(2,1)S(1)}, bf16[96,4096]{1,0:T(8,128)(2,1)S(1)}, u32[]{:S(2)}, u32[]{:S(2)}) collective-permute-start(bf16[96,4096]{1,0:T(8,128)(2,1)S(1)} %broadcast_select_fusion.1), channel_id=1, source_target_pairs={{0,224},{4,228},{8,232},{12,236},{16,240},{20,244},{24,248},{28,25... | collective-permute-start | bytes 2359304 | tf_op jit(solution)/shard_map/ppermute | solution.py:32
  117.6 4.3 %copy-start.13 = (f32[96,4096]{1,0:T(8,128)}, f32[96,4096]{1,0:T(8,128)S(1)}, u32[]{:S(2)}) copy-start(f32[96,4096]{1,0:T(8,128)S(1)} %get-tuple-element.43) | copy-start | bytes 4718596
  121.1 7.5 %collective-permute-start.14 = (bf16[48,4096]{1,0:T(8,128)(2,1)S(1)}, bf16[48,4096]{1,0:T(8,128)(2,1)S(1)}, u32[]{:S(2)}, u32[]{:S(2)}) collective-permute-start(bf16[48,4096]{1,0:T(8,128)(2,1)S(1)} %slice.52), channel_id=1, source_target_pairs={{0,32},{4,36},{8,40},{12,44},{16,48},{20,52},{24,56},{28,60},{1,33... | collective-permute-start | bytes 1179656 | tf_op jit(solution)/shard_map/ppermute | solution.py:32
  121.9 6.7 %collective-permute-start.11 = (bf16[48,4096]{1,0:T(8,128)(2,1)S(1)}, bf16[48,4096]{1,0:T(8,128)(2,1)S(1)}, u32[]{:S(2)}, u32[]{:S(2)}) collective-permute-start(bf16[48,4096]{1,0:T(8,128)(2,1)S(1)} %slice.64), channel_id=1, source_target_pairs={{0,224},{4,228},{8,232},{12,236},{16,240},{20,244},{24,248},{28,25... | collective-permute-start | bytes 1179656 | tf_op jit(solution)/shard_map/ppermute | solution.py:32
  128.6 5.6 %copy-start.5 = (f32[96,4096]{1,0:T(8,128)}, f32[96,4096]{1,0:T(8,128)S(1)}, u32[]{:S(2)}) copy-start(f32[96,4096]{1,0:T(8,128)S(1)} %get-tuple-element.40) | copy-start | bytes 4718596
  135.6 12.4 %collective-permute-start.15 = (bf16[96,4096]{1,0:T(8,128)(2,1)}, bf16[96,4096]{1,0:T(8,128)(2,1)}, u32[]{:S(2)}, u32[]{:S(2)}) collective-permute-start(bf16[96,4096]{1,0:T(8,128)(2,1)} %get-tuple-element.59), channel_id=1, source_target_pairs={{0,32},{4,36},{8,40},{12,44},{16,48},{20,52},{24,56},{28,60},{1,33... | collective-permute-start | bytes 2359304 | tf_op jit(solution)/shard_map/ppermute | solution.py:32
  137.7 12.0 %copy-start.14 = (f32[96,4096]{1,0:T(8,128)S(1)}, f32[96,4096]{1,0:T(8,128)}, u32[]{:S(2)}) copy-start(f32[96,4096]{1,0:T(8,128)} %copy-done.13) | copy-start | bytes 4718596
  137.7 12.0 %collective-permute-start.17 = (bf16[96,4096]{1,0:T(8,128)(2,1)}, bf16[96,4096]{1,0:T(8,128)(2,1)S(1)}, u32[]{:S(2)}, u32[]{:S(2)}) collective-permute-start(bf16[96,4096]{1,0:T(8,128)(2,1)} %get-tuple-element.60), channel_id=1, source_target_pairs={{0,224},{4,228},{8,232},{12,236},{16,240},{20,244},{24,248},{28,25... | collective-permute-start | bytes 2359304 | tf_op jit(solution)/shard_map/ppermute | solution.py:32
  149.4 12.7 %copy-start.6 = (f32[96,4096]{1,0:T(8,128)S(1)}, f32[96,4096]{1,0:T(8,128)}, u32[]{:S(2)}) copy-start(f32[96,4096]{1,0:T(8,128)} %copy-done.5) | copy-start | bytes 4718596
  149.4 12.6 %collective-permute-start.16 = (bf16[96,4096]{1,0:T(8,128)(2,1)S(1)}, bf16[96,4096]{1,0:T(8,128)(2,1)S(1)}, u32[]{:S(2)}, u32[]{:S(2)}) collective-permute-start(bf16[96,4096]{1,0:T(8,128)(2,1)S(1)} %add_convert_fusion.3), channel_id=1, source_target_pairs={{0,32},{4,36},{8,40},{12,44},{16,48},{20,52},{24,56},{28,60},{1,33... | collective-permute-start | bytes 2359304 | tf_op jit(solution)/shard_map/ppermute | solution.py:32
  149.9 12.5 %collective-permute-start.18 = (bf16[96,4096]{1,0:T(8,128)(2,1)S(1)}, bf16[96,4096]{1,0:T(8,128)(2,1)S(1)}, u32[]{:S(2)}, u32[]{:S(2)}) collective-permute-start(bf16[96,4096]{1,0:T(8,128)(2,1)S(1)} %add_convert_fusion.2), channel_id=1, source_target_pairs={{0,224},{4,228},{8,232},{12,236},{16,240},{20,244},{24,248},{28,25... | collective-permute-start | bytes 2359304 | tf_op jit(solution)/shard_map/ppermute | solution.py:32
  162.3 12.4 %collective-permute-start.22 = (bf16[96,4096]{1,0:T(8,128)(2,1)S(1)}, bf16[96,4096]{1,0:T(8,128)(2,1)S(1)}, u32[]{:S(2)}, u32[]{:S(2)}) collective-permute-start(bf16[96,4096]{1,0:T(8,128)(2,1)S(1)} %select_convert_fusion), channel_id=1, source_target_pairs={{0,32},{4,36},{8,40},{12,44},{16,48},{20,52},{24,56},{28,60},{1,33... | collective-permute-start | bytes 2359304 | tf_op jit(solution)/shard_map/ppermute | solution.py:32
  162.4 8.9 %copy-start.10 = (f32[96,4096]{1,0:T(8,128)S(1)}, f32[96,4096]{1,0:T(8,128)}, u32[]{:S(2)}) copy-start(f32[96,4096]{1,0:T(8,128)} %copy-done.9) | copy-start | bytes 4718596
  162.8 12.2 %collective-permute-start.21 = (bf16[24,4096]{1,0:T(8,128)(2,1)S(1)}, bf16[24,4096]{1,0:T(8,128)(2,1)S(1)}, u32[]{:S(2)}, u32[]{:S(2)}) collective-permute-start(bf16[24,4096]{1,0:T(8,128)(2,1)S(1)} %get-tuple-element.63), channel_id=1, source_target_pairs={{2,226},{6,230},{10,234},{14,238},{18,242},{22,246},{26,250},{30,2... | collective-permute-start | bytes 589832 | tf_op jit(solution)/shard_map/ppermute | solution.py:32
  166.1 11.6 %collective-permute-start.20 = (bf16[24,4096]{1,0:T(8,128)(2,1)S(1)}, bf16[24,4096]{1,0:T(8,128)(2,1)S(1)}, u32[]{:S(2)}, u32[]{:S(2)}) collective-permute-start(bf16[24,4096]{1,0:T(8,128)(2,1)S(1)} %get-tuple-element.64), channel_id=1, source_target_pairs={{2,194},{6,198},{10,202},{14,206},{18,210},{22,214},{26,218},{30,2... | collective-permute-start | bytes 589832 | tf_op jit(solution)/shard_map/ppermute | solution.py:32
  168.0 6.7 %copy-start.12 = (f32[96,4096]{1,0:T(8,128)S(1)}, f32[96,4096]{1,0:T(8,128)}, u32[]{:S(2)}) copy-start(f32[96,4096]{1,0:T(8,128)} %copy-done.11) | copy-start | bytes 4718596
  168.0 9.6 %collective-permute-start.19 = (bf16[24,4096]{1,0:T(8,128)(2,1)S(1)}, bf16[24,4096]{1,0:T(8,128)(2,1)S(1)}, u32[]{:S(2)}, u32[]{:S(2)}) collective-permute-start(bf16[24,4096]{1,0:T(8,128)(2,1)S(1)} %get-tuple-element.65), channel_id=1, source_target_pairs={{2,34},{6,38},{10,42},{14,46},{18,50},{22,54},{26,58},{30,62},{3,3... | collective-permute-start | bytes 589832 | tf_op jit(solution)/shard_map/ppermute | solution.py:32
  171.4 8.3 %copy-start.16 = (bf16[3,8,16,256]{3,1,2,0:T(8,128)(2,1)S(1)}, bf16[3,8,16,256]{3,1,2,0:T(8,128)(2,1)}, u32[]{:S(2)}) copy-start(bf16[3,8,16,256]{3,1,2,0:T(8,128)(2,1)} %copy-done.15) | copy-start | bytes 589828
  171.4 8.3 %copy-start.20 = (bf16[4096,8]{0,1:T(8,128)(2,1)S(1)}, bf16[4096,8]{0,1:T(8,128)(2,1)}, u32[]{:S(2)}) copy-start(bf16[4096,8]{0,1:T(8,128)(2,1)} %param.14) | copy-start | bytes 196612
  171.4 15.9 %copy-start.8 = (f32[96,4096]{1,0:T(8,128)S(1)}, f32[96,4096]{1,0:T(8,128)}, u32[]{:S(2)}) copy-start(f32[96,4096]{1,0:T(8,128)} %copy-done.7) | copy-start | bytes 4718596
  171.4 15.9 %collective-permute-start.25 = (bf16[96,4096]{1,0:T(8,128)(2,1)S(1)}, bf16[96,4096]{1,0:T(8,128)(2,1)S(1)}, u32[]{:S(2)}, u32[]{:S(2)}) collective-permute-start(bf16[96,4096]{1,0:T(8,128)(2,1)S(1)} %add_convert_fusion), channel_id=1, source_target_pairs={{0,224},{4,228},{8,232},{12,236},{16,240},{20,244},{24,248},{28,25... | collective-permute-start | bytes 2359304 | tf_op jit(solution)/shard_map/ppermute | solution.py:32
  174.9 12.4 %collective-permute-start.24 = (bf16[96,4096]{1,0:T(8,128)(2,1)S(1)}, bf16[96,4096]{1,0:T(8,128)(2,1)S(1)}, u32[]{:S(2)}, u32[]{:S(2)}) collective-permute-start(bf16[96,4096]{1,0:T(8,128)(2,1)S(1)} %add_convert_fusion.1), channel_id=1, source_target_pairs={{0,32},{4,36},{8,40},{12,44},{16,48},{20,52},{24,56},{28,60},{1,33... | collective-permute-start | bytes 2359304 | tf_op jit(solution)/shard_map/ppermute | solution.py:32
  177.7 9.2 %collective-permute-start.23 = (bf16[24,4096]{1,0:T(8,128)(2,1)S(1)}, bf16[24,4096]{1,0:T(8,128)(2,1)S(1)}, u32[]{:S(2)}, u32[]{:S(2)}) collective-permute-start(bf16[24,4096]{1,0:T(8,128)(2,1)S(1)} %fusion.17), channel_id=1, source_target_pairs={{2,194},{6,198},{10,202},{14,206},{18,210},{22,214},{26,218},{30,2... | collective-permute-start | bytes 589832 | tf_op jit(solution)/shard_map/ppermute | solution.py:32
  187.8 24.8 %copy-start.18 = (bf16[128,256]{1,0:T(8,128)(2,1)S(1)}, bf16[128,256]{1,0:T(8,128)(2,1)}, u32[]{:S(2)}) copy-start(bf16[128,256]{1,0:T(8,128)(2,1)} %param.12) | copy-start | bytes 196612
  187.8 9.1 %collective-permute-start.28 = (bf16[24,4096]{1,0:T(8,128)(2,1)S(1)}, bf16[24,4096]{1,0:T(8,128)(2,1)S(1)}, u32[]{:S(2)}, u32[]{:S(2)}) collective-permute-start(bf16[24,4096]{1,0:T(8,128)(2,1)S(1)} %fusion.10), channel_id=1, source_target_pairs={{0,1},{4,5},{8,9},{12,13},{16,17},{20,21},{24,25},{28,29},{1,0},{5... | collective-permute-start | bytes 589832 | tf_op jit(solution)/shard_map/ppermute | solution.py:32
  190.0 7.7 %collective-permute-start.26 = (bf16[24,4096]{1,0:T(8,128)(2,1)S(1)}, bf16[24,4096]{1,0:T(8,128)(2,1)S(1)}, u32[]{:S(2)}, u32[]{:S(2)}) collective-permute-start(bf16[24,4096]{1,0:T(8,128)(2,1)S(1)} %get-tuple-element.61), channel_id=1, source_target_pairs={{0,16},{4,20},{8,24},{12,28},{16,1},{20,5},{24,9},{28,13},{1,17},{... | collective-permute-start | bytes 589832 | tf_op jit(solution)/shard_map/ppermute | solution.py:32
  190.3 7.4 %collective-permute-start.27 = (bf16[24,4096]{1,0:T(8,128)(2,1)S(1)}, bf16[24,4096]{1,0:T(8,128)(2,1)S(1)}, u32[]{:S(2)}, u32[]{:S(2)}) collective-permute-start(bf16[24,4096]{1,0:T(8,128)(2,1)S(1)} %get-tuple-element.62), channel_id=1, source_target_pairs={{0,17},{4,21},{8,25},{12,29},{16,0},{20,4},{24,8},{28,12},{1,16},{... | collective-permute-start | bytes 589832 | tf_op jit(solution)/shard_map/ppermute | solution.py:32
  (4 other events, 5.8 us)

commit v3 on v2

--- a/solution.py
+++ b/solution.py
@@ -237,15 +237,16 @@
     plus_2 = hop(b16(go_plus), (1, 0), (0, 1))
     minus_3 = hop(b16(sums[1][1] + f32(minus_2)), (-1, 0), None)
     plus_3 = hop(b16(pick(sums[2][0] + f32(plus_2), sums[3][0])), (1, 0), (0, 1))
-    both = lax.optimization_barrier((plus_2, minus_2))
+    both = lax.optimization_barrier((plus_2, minus_2, plus_3))
     rest = sum_last + f32(both[0]) + f32(both[1])
     rest = [rest[k * n : (k + 1) * n] for k in range(4)]
     from_1, from_2 = hop(b16(rest[1]), None, (1, 0)), hop(b16(rest[3]), None, (-2, 0))
     from_above = hop(b16(rest[2]), None, (-1, 0))
-    from_1, from_2, from_above, _ = lax.optimization_barrier((from_1, from_2, from_above, plus_3))
     plus_4 = hop(b16(sums[1][0] + f32(plus_3)), (1, 0), (0, 1))
+    from_1, from_2, from_above, plus_4 = lax.optimization_barrier(
+        (from_1, from_2, from_above, plus_4)
+    )
     last_down = hop(b16(rest[0] + f32(from_above) + f32(from_2)), None, (-2, 0))
-    last_down, plus_4 = lax.optimization_barrier((last_down, plus_4))
     total = sum_own + f32(plus_4) + f32(pick(minus_3, minus_1))
     chunk = [total[k * n : (k + 1) * n] for k in range(4)]
     result = chunk[0] + f32(last_down)

time: 214 us -> 225 us (1.051)
  blocking collectives: 14.7 us -> 19 us
  waiting for transfers between devices: 75.5 us -> 79.4 us
    all_to_all x1, blocking collectives: 14.7 us -> 19 us  [shards(): lax.all_to_all(back, ('expert', 'ffn'), split_axis=1, concat_axis=0, tile...]
    ppermute x29, waiting for transfers between devices: 43.8 us -> 47.6 us  [hop(): return lax.ppermute(value, ALL, pairs)]
    unnamed x50 -> x44, local copies, waits for them, and re-layouts: 8.44 us -> 8.45 us
  transfers between devices with their start and end apart: 31 -> 31, of which waited for: 13 -> 14; matrix products, arithmetic and copies ran while one was open for 3% -> 4% of each run, Pallas kernels for 11% -> 10%
where the time goes in v3:
time: 225 us
  waiting for transfers between devices  79.4 us (35%)
  starting transfers between devices  70.4 us (31%)
  Pallas kernels  28.5 us (13%)
  blocking collectives  19 us (8%)
  local copies, waits for them, and re-layouts  12.3 us (5%)
  other arithmetic  9.5 us (4%)
  matrix products  4.69 us (2%)
    ppermute x29, starting transfers between devices, hop(): return lax.ppermute(value, ALL, pairs)  49.4 us
    ppermute x29, waiting for transfers between devices, hop(): return lax.ppermute(value, ALL, pairs)  47.6 us
    pallas_call x5, Pallas kernels, expert(): pl.pallas_call(functools.partial(expert_kernel, tuple(places), tuple(outs...  28.5 us
    all_to_all x1, waiting for transfers between devices, shards(): lax.all_to_all(jnp.broadcast_to(pair[None], (n_seq,) + pair.shape), 'seq'...  23.5 us
    all_to_all x1, blocking collectives, shards(): lax.all_to_all(back, ('expert', 'ffn'), split_axis=1, concat_axis=0, tile...  19 us
    all_to_all x1, starting transfers between devices, shards(): lax.all_to_all(send, ('expert', 'ffn'), split_axis=0, concat_axis=2, tile...  11 us
    all_to_all x1, starting transfers between devices, shards(): lax.all_to_all(jnp.broadcast_to(pair[None], (n_seq,) + pair.shape), 'seq'...  10 us
    unnamed x44, local copies, waits for them, and re-layouts  8.45 us
  transfers between devices with their start and end apart: 31, of which 14 were waited for; matrix products, arithmetic and copies ran while one was open for 4% of the time, Pallas kernels for 10%

profile of v3, /device:TPU:1, one launch (start us, length us, event | category | flops | bytes accessed | tf_op | source)
XLA Modules:
  0.0 224.6 jit_solution(14232868946177634697)
XLA Ops:
  0.8 1.1 broadcast_in_dim.52
  1.9 10.0 %all-to-all-start = ((bf16[16,128,256]{2,1,0:T(8,128)(2,1)}), bf16[16,128,256]{2,1,0:T(8,128)(2,1)S(1)}, u32[]{:S(2)}, u32[]{:S(2)}) async-start(bf16[16,128,256]{2,1,0:T(8,128)(2,1)} %broadcast_in_dim.52), calls=%async_computation | async-start | bytes 2097152 | tf_op jit(solution)/shard_map/all_to_all | solution.py:154
  13.8 23.5 %all-to-all-done = bf16[16,128,256]{2,1,0:T(8,128)(2,1)S(1)} async-done(((bf16[16,128,256]{2,1,0:T(8,128)(2,1)}), bf16[16,128,256]{2,1,0:T(8,128)(2,1)S(1)}, u32[]{:S(2)}, u32[]{:S(2)}) %all-to-all-start) | async-done | bytes 1048608 | tf_op jit(solution)/shard_map/all_to_all | solution.py:154
  38.2 1.3 fusion.5
  40.5 11.0 %all-to-all-start.1 = ((bf16[16,24,1,256]{3,1,2,0:T(8,128)(2,1)}), bf16[16,24,1,256]{3,1,2,0:T(8,128)(2,1)S(1)}, u32[]{:S(2)}, u32[]{:S(2)}) async-start(bf16[16,24,1,256]{3,1,2,0:T(8,128)(2,1)} %bitcast.10), calls=%async_computation.1 | async-start | bytes 393216 | tf_op jit(solution)/shard_map/all_to_all | solution.py:174
  51.5 8.3 %all-to-all-done.1 = bf16[16,24,1,256]{3,1,2,0:T(8,128)(2,1)S(1)} async-done(((bf16[16,24,1,256]{3,1,2,0:T(8,128)(2,1)}), bf16[16,24,1,256]{3,1,2,0:T(8,128)(2,1)S(1)}, u32[]{:S(2)}, u32[]{:S(2)}) %all-to-all-start.1) | async-done | bytes 196640 | tf_op jit(solution)/shard_map/all_to_all | solution.py:174
  59.8 2.0 collective-permute-start.5
  61.9 3.5 %collective-permute-start.2 = (bf16[24,4096]{1,0:T(8,128)(2,1)S(1)}, bf16[24,4096]{1,0:T(8,128)(2,1)S(1)}, u32[]{:S(2)}, u32[]{:S(2)}) collective-permute-start(bf16[24,4096]{1,0:T(8,128)(2,1)S(1)} %bitcast.88), channel_id=1, source_target_pairs={{0,1},{4,5},{8,9},{12,13},{16,17},{20,21},{24,25},{28,29},{1,0},{5... | collective-permute-start | bytes 589832 | tf_op jit(solution)/shard_map/ppermute | solution.py:32
  65.4 2.7 %collective-permute-start = (bf16[24,4096]{1,0:T(8,128)(2,1)S(1)}, bf16[24,4096]{1,0:T(8,128)(2,1)S(1)}, u32[]{:S(2)}, u32[]{:S(2)}) collective-permute-start(bf16[24,4096]{1,0:T(8,128)(2,1)S(1)} %bitcast.90), channel_id=1, source_target_pairs={{0,17},{4,21},{8,25},{12,29},{16,0},{20,4},{24,8},{28,12},{1,16},{... | collective-permute-start | bytes 589832 | tf_op jit(solution)/shard_map/ppermute | solution.py:32
  68.1 3.5 %collective-permute-done = bf16[24,4096]{1,0:T(8,128)(2,1)S(1)} collective-permute-done((bf16[24,4096]{1,0:T(8,128)(2,1)S(1)}, bf16[24,4096]{1,0:T(8,128)(2,1)S(1)}, u32[]{:S(2)}, u32[]{:S(2)}) %collective-permute-start) | collective-permute-done | bytes 196640 | tf_op jit(solution)/shard_map/ppermute | solution.py:32
  71.8 1.5 collective-permute-start.3
  73.3 5.2 %collective-permute-start.8 = (bf16[24,4096]{1,0:T(8,128)(2,1)S(1)}, bf16[24,4096]{1,0:T(8,128)(2,1)S(1)}, u32[]{:S(2)}, u32[]{:S(2)}) collective-permute-start(bf16[24,4096]{1,0:T(8,128)(2,1)S(1)} %collective-permute-done.2), channel_id=1, source_target_pairs={{2,194},{6,198},{10,202},{14,206},{18,210},{22,214},{26,218},{30,2... | collective-permute-start | bytes 589832 | tf_op jit(solution)/shard_map/ppermute | solution.py:32
  78.5 2.0 collective-permute-start.6
  80.5 3.3 %collective-permute-start.7 = (bf16[24,4096]{1,0:T(8,128)(2,1)S(1)}, bf16[24,4096]{1,0:T(8,128)(2,1)S(1)}, u32[]{:S(2)}, u32[]{:S(2)}) collective-permute-start(bf16[24,4096]{1,0:T(8,128)(2,1)S(1)} %collective-permute-done.5), channel_id=1, source_target_pairs={{2,34},{6,38},{10,42},{14,46},{18,50},{22,54},{26,58},{30,62},{3,3... | collective-permute-start | bytes 589832 | tf_op jit(solution)/shard_map/ppermute | solution.py:32
  83.8 2.0 copy-done.1
  85.9 2.0 copy-done.3
  87.9 2.0 copy-done.4
  89.9 5.3 %shard_map.91 = f32[96,4096]{1,0:T(8,128)S(1)} custom-call(bf16[96,4096]{1,0:T(8,128)(2,1)S(1)} %constant_dynamic-update-slice_fusion.refs_0_, bf16[448,4096]{1,0:T(8,128)(2,1)S(1)} %bitcast.69, bf16[448,4096]{1,0:T(8,128)(2,1)S(1)} %bitcast.74, bf16[448,4096]{1,0:T(8,128)(2,1)S(1)} %bitcast.79), custom_call_target="tpu_custom_call" | custom-call | flops 1056964608 | bytes 13369344 | tf_op jit(solution)/shard_map/pallas_call | solution.py:98
  96.4 2.7 %collective-permute-start.9 = (bf16[96,4096]{1,0:T(8,128)(2,1)S(1)}, bf16[96,4096]{1,0:T(8,128)(2,1)S(1)}, u32[]{:S(2)}, u32[]{:S(2)}) collective-permute-start(bf16[96,4096]{1,0:T(8,128)(2,1)S(1)} %get-tuple-element.64), channel_id=1, source_target_pairs={{0,224},{4,228},{8,232},{12,236},{16,240},{20,244},{24,248},{28,25... | collective-permute-start | bytes 2359304 | tf_op jit(solution)/shard_map/ppermute | solution.py:32
  99.1 6.0 %shard_map.92 = (f32[96,4096]{1,0:T(8,128)S(1)}, f32[96,4096]{1,0:T(8,128)S(1)}) custom-call(bf16[96,4096]{1,0:T(8,128)(2,1)S(1)} %collective-permute-done.4.refs_0_, bf16[96,4096]{1,0:T(8,128)(2,1)S(1)} %collective-permute-done.3.refs_1_, bf16[448,4096]{1,0:T(8,128)(2,1)S(1)} %bitcast.70, bf16[448,4096]{1,0:T(8,128)(2,1)S(1)} %bitcast.75, ...), custom_call_target="tpu_custom_call" | custom-call | flops 2113929216 | bytes 15728640 | tf_op jit(solution)/shard_map/pallas_call | solution.py:98
  105.1 1.2 copy-done.10
  106.3 2.5 %collective-permute-done.12.refs_1_ = bf16[96,4096]{1,0:T(8,128)(2,1)S(1)} collective-permute-done((bf16[96,4096]{1,0:T(8,128)(2,1)S(1)}, bf16[96,4096]{1,0:T(8,128)(2,1)S(1)}, u32[]{:S(2)}, u32[]{:S(2)}) %collective-permute-start.12) | collective-permute-done | bytes 786464 | tf_op jit(solution)/shard_map/ppermute | solution.py:32
  108.9 2.8 %collective-permute-start.10 = (bf16[96,4096]{1,0:T(8,128)(2,1)S(1)}, bf16[96,4096]{1,0:T(8,128)(2,1)S(1)}, u32[]{:S(2)}, u32[]{:S(2)}) collective-permute-start(bf16[96,4096]{1,0:T(8,128)(2,1)S(1)} %broadcast_select_fusion.1), channel_id=1, source_target_pairs={{0,224},{4,228},{8,232},{12,236},{16,240},{20,244},{24,248},{28,25... | collective-permute-start | bytes 2359304 | tf_op jit(solution)/shard_map/ppermute | solution.py:32
  111.6 6.0 %shard_map.93 = (f32[96,4096]{1,0:T(8,128)S(1)}, f32[96,4096]{1,0:T(8,128)S(1)}) custom-call(bf16[96,4096]{1,0:T(8,128)(2,1)S(1)} %collective-permute-done.9.refs_0_, bf16[96,4096]{1,0:T(8,128)(2,1)S(1)} %collective-permute-done.12.refs_1_, bf16[448,4096]{1,0:T(8,128)(2,1)S(1)} %bitcast.71, bf16[448,4096]{1,0:T(8,128)(2,1)S(1)} %bitcast.76, ...), custom_call_target="tpu_custom_call" | custom-call | flops 2113929216 | bytes 15728640 | tf_op jit(solution)/shard_map/pallas_call | solution.py:98
  117.6 3.5 %collective-permute-done.13.refs_1_ = bf16[96,4096]{1,0:T(8,128)(2,1)S(1)} collective-permute-done((bf16[96,4096]{1,0:T(8,128)(2,1)S(1)}, bf16[96,4096]{1,0:T(8,128)(2,1)S(1)}, u32[]{:S(2)}, u32[]{:S(2)}) %collective-permute-start.13) | collective-permute-done | bytes 786464 | tf_op jit(solution)/shard_map/ppermute | solution.py:32
  122.6 6.0 %shard_map.94 = (f32[96,4096]{1,0:T(8,128)S(1)}, f32[96,4096]{1,0:T(8,128)S(1)}) custom-call(bf16[96,4096]{1,0:T(8,128)(2,1)S(1)} %collective-permute-done.10.refs_0_, bf16[96,4096]{1,0:T(8,128)(2,1)S(1)} %collective-permute-done.13.refs_1_, bf16[448,4096]{1,0:T(8,128)(2,1)S(1)} %bitcast.72, bf16[448,4096]{1,0:T(8,128)(2,1)S(1)} %bitcast.77, ...), custom_call_target="tpu_custom_call" | custom-call | flops 2113929216 | bytes 15728640 | tf_op jit(solution)/shard_map/pallas_call | solution.py:98
  128.8 5.3 %shard_map.95 = f32[96,4096]{1,0:T(8,128)S(1)} custom-call(bf16[96,4096]{1,0:T(8,128)(2,1)S(1)} %maximum_select_fusion.refs_0_, bf16[448,4096]{1,0:T(8,128)(2,1)S(1)} %bitcast.73, bf16[448,4096]{1,0:T(8,128)(2,1)S(1)} %bitcast.78, bf16[448,4096]{1,0:T(8,128)(2,1)S(1)} %bitcast.83), custom_call_target="tpu_custom_call" | custom-call | flops 1056964608 | bytes 13369344 | tf_op jit(solution)/shard_map/pallas_call | solution.py:98
  134.2 1.2 select_convert_fusion.2
  135.3 12.0 %collective-permute-done.15 = bf16[96,4096]{1,0:T(8,128)(2,1)S(1)} collective-permute-done((bf16[96,4096]{1,0:T(8,128)(2,1)S(1)}, bf16[96,4096]{1,0:T(8,128)(2,1)S(1)}, u32[]{:S(2)}, u32[]{:S(2)}) %collective-permute-start.15) | collective-permute-done | bytes 786464 | tf_op jit(solution)/shard_map/ppermute | solution.py:32
  147.4 1.1 add_convert_fusion.3
  150.5 1.1 select_reduce_fusion.1
  151.6 3.0 %collective-permute-start.17 = (bf16[96,4096]{1,0:T(8,128)(2,1)}, bf16[96,4096]{1,0:T(8,128)(2,1)S(1)}, u32[]{:S(2)}, u32[]{:S(2)}) collective-permute-start(bf16[96,4096]{1,0:T(8,128)(2,1)} %get-tuple-element.58), channel_id=1, source_target_pairs={{0,224},{4,228},{8,232},{12,236},{16,240},{20,244},{24,248},{28,25... | collective-permute-start | bytes 2359304 | tf_op jit(solution)/shard_map/ppermute | solution.py:32
  154.6 6.2 %collective-permute-done.16 = bf16[96,4096]{1,0:T(8,128)(2,1)} collective-permute-done((bf16[96,4096]{1,0:T(8,128)(2,1)}, bf16[96,4096]{1,0:T(8,128)(2,1)}, u32[]{:S(2)}, u32[]{:S(2)}) %collective-permute-start.16) | collective-permute-done | bytes 786464 | tf_op jit(solution)/shard_map/ppermute | solution.py:32
  160.8 1.8 select_convert_fusion
  162.8 1.1 collective-permute-done.17
  164.1 3.1 %collective-permute-start.18 = (bf16[96,4096]{1,0:T(8,128)(2,1)S(1)}, bf16[96,4096]{1,0:T(8,128)(2,1)S(1)}, u32[]{:S(2)}, u32[]{:S(2)}) collective-permute-start(bf16[96,4096]{1,0:T(8,128)(2,1)S(1)} %add_convert_fusion.2), channel_id=1, source_target_pairs={{0,224},{4,228},{8,232},{12,236},{16,240},{20,244},{24,248},{28,25... | collective-permute-start | bytes 2359304 | tf_op jit(solution)/shard_map/ppermute | solution.py:32
  167.2 7.9 %collective-permute-done.19 = bf16[96,4096]{1,0:T(8,128)(2,1)S(1)} collective-permute-done((bf16[96,4096]{1,0:T(8,128)(2,1)S(1)}, bf16[96,4096]{1,0:T(8,128)(2,1)S(1)}, u32[]{:S(2)}, u32[]{:S(2)}) %collective-permute-start.19) | collective-permute-done | bytes 786464 | tf_op jit(solution)/shard_map/ppermute | solution.py:32
  176.1 1.5 fusion.29
  177.7 3.2 %collective-permute-start.22 = (bf16[24,4096]{1,0:T(8,128)(2,1)S(1)}, bf16[24,4096]{1,0:T(8,128)(2,1)S(1)}, u32[]{:S(2)}, u32[]{:S(2)}) collective-permute-start(bf16[24,4096]{1,0:T(8,128)(2,1)S(1)} %get-tuple-element.61), channel_id=1, source_target_pairs={{2,226},{6,230},{10,234},{14,238},{18,242},{22,246},{26,250},{30,2... | collective-permute-start | bytes 589832 | tf_op jit(solution)/shard_map/ppermute | solution.py:32
  180.9 1.9 collective-permute-start.21
  182.9 3.2 %collective-permute-start.20 = (bf16[24,4096]{1,0:T(8,128)(2,1)S(1)}, bf16[24,4096]{1,0:T(8,128)(2,1)S(1)}, u32[]{:S(2)}, u32[]{:S(2)}) collective-permute-start(bf16[24,4096]{1,0:T(8,128)(2,1)S(1)} %get-tuple-element.63), channel_id=1, source_target_pairs={{2,34},{6,38},{10,42},{14,46},{18,50},{22,54},{26,58},{30,62},{3,3... | collective-permute-start | bytes 589832 | tf_op jit(solution)/shard_map/ppermute | solution.py:32
  187.0 5.4 %collective-permute-done.21 = bf16[24,4096]{1,0:T(8,128)(2,1)S(1)} collective-permute-done((bf16[24,4096]{1,0:T(8,128)(2,1)S(1)}, bf16[24,4096]{1,0:T(8,128)(2,1)S(1)}, u32[]{:S(2)}, u32[]{:S(2)}) %collective-permute-start.21) | collective-permute-done | bytes 196640 | tf_op jit(solution)/shard_map/ppermute | solution.py:32
  192.5 1.9 collective-permute-start.25
  194.9 2.4 %collective-permute-start.28 = (bf16[24,4096]{1,0:T(8,128)(2,1)S(1)}, bf16[24,4096]{1,0:T(8,128)(2,1)S(1)}, u32[]{:S(2)}, u32[]{:S(2)}) collective-permute-start(bf16[24,4096]{1,0:T(8,128)(2,1)S(1)} %fusion.10), channel_id=1, source_target_pairs={{0,1},{4,5},{8,9},{12,13},{16,17},{20,21},{24,25},{28,29},{1,0},{5... | collective-permute-start | bytes 589832 | tf_op jit(solution)/shard_map/ppermute | solution.py:32
  197.3 2.7 %collective-permute-start.27 = (bf16[24,4096]{1,0:T(8,128)(2,1)S(1)}, bf16[24,4096]{1,0:T(8,128)(2,1)S(1)}, u32[]{:S(2)}, u32[]{:S(2)}) collective-permute-start(bf16[24,4096]{1,0:T(8,128)(2,1)S(1)} %get-tuple-element.60), channel_id=1, source_target_pairs={{0,17},{4,21},{8,25},{12,29},{16,0},{20,4},{24,8},{28,12},{1,16},{... | collective-permute-start | bytes 589832 | tf_op jit(solution)/shard_map/ppermute | solution.py:32
  200.0 2.3 %collective-permute-done.25 = bf16[24,4096]{1,0:T(8,128)(2,1)S(1)} collective-permute-done((bf16[24,4096]{1,0:T(8,128)(2,1)S(1)}, bf16[24,4096]{1,0:T(8,128)(2,1)S(1)}, u32[]{:S(2)}, u32[]{:S(2)}) %collective-permute-start.25) | collective-permute-done | bytes 196640 | tf_op jit(solution)/shard_map/ppermute | solution.py:32
  202.6 2.0 collective-permute-done.26
  204.8 19.0 %all_to_all.35 = bf16[24,16,256]{2,0,1:T(8,128)(2,1)S(1)} all-to-all(bf16[24,16,256]{2,0,1:T(8,128)(2,1)S(1)} %bitcast.94), channel_id=1, replica_groups=mesh['seq'=16,'expert'=8,'ffn'=2] {'expert','ffn'}, dimensions={1} | all-to-all | bytes 393216 | tf_op jit(solution)/shard_map/all_to_all | solution.py:258
  (117 shorter events, 13.6 us)
Async XLA Ops:
  0.0 37.3 %copy-start = (bf16[128,256]{1,0:T(8,128)(2,1)S(1)}, bf16[128,256]{1,0:T(8,128)(2,1)}, u32[]{:S(2)}) copy-start(bf16[128,256]{1,0:T(8,128)(2,1)} %param.9) | copy-start | bytes 196612
  0.8 11.1 %copy-start.17 = (s32[128,2]{0,1:T(2,128)S(1)}, s32[128,2]{0,1:T(2,128)}, u32[]{:S(2)}) copy-start(s32[128,2]{0,1:T(2,128)} %param.13) | copy-start | bytes 3076
  1.9 35.4 %all-to-all-start = ((bf16[16,128,256]{2,1,0:T(8,128)(2,1)}), bf16[16,128,256]{2,1,0:T(8,128)(2,1)S(1)}, u32[]{:S(2)}, u32[]{:S(2)}) async-start(bf16[16,128,256]{2,1,0:T(8,128)(2,1)} %broadcast_in_dim.52), calls=%async_computation | async-start | bytes 2097152 | tf_op jit(solution)/shard_map/all_to_all | solution.py:154
  38.2 1.4 copy-start.15
  40.5 19.3 %all-to-all-start.1 = ((bf16[16,24,1,256]{3,1,2,0:T(8,128)(2,1)}), bf16[16,24,1,256]{3,1,2,0:T(8,128)(2,1)S(1)}, u32[]{:S(2)}, u32[]{:S(2)}) async-start(bf16[16,24,1,256]{3,1,2,0:T(8,128)(2,1)} %bitcast.10), calls=%async_computation.1 | async-start | bytes 393216 | tf_op jit(solution)/shard_map/all_to_all | solution.py:174
  59.8 35.4 %copy-start.14 = (bf16[3,8,16,256]{3,1,2,0:T(8,128)(2,1)}, bf16[3,8,16,256]{3,1,2,0:T(8,128)(2,1)S(1)}, u32[]{:S(2)}) copy-start(bf16[3,8,16,256]{3,1,2,0:T(8,128)(2,1)S(1)} %copy.68) | copy-start | bytes 589828
  59.8 20.7 %collective-permute-start.5 = (bf16[24,4096]{1,0:T(8,128)(2,1)S(1)}, bf16[24,4096]{1,0:T(8,128)(2,1)S(1)}, u32[]{:S(2)}, u32[]{:S(2)}) collective-permute-start(bf16[24,4096]{1,0:T(8,128)(2,1)S(1)} %bitcast.87), channel_id=1, source_target_pairs={{2,66},{6,70},{10,74},{14,78},{18,82},{22,86},{26,90},{30,94},{3,6... | collective-permute-start | bytes 589832 | tf_op jit(solution)/shard_map/ppermute | solution.py:32
  61.9 9.8 %collective-permute-start.2 = (bf16[24,4096]{1,0:T(8,128)(2,1)S(1)}, bf16[24,4096]{1,0:T(8,128)(2,1)S(1)}, u32[]{:S(2)}, u32[]{:S(2)}) collective-permute-start(bf16[24,4096]{1,0:T(8,128)(2,1)S(1)} %bitcast.88), channel_id=1, source_target_pairs={{0,1},{4,5},{8,9},{12,13},{16,17},{20,21},{24,25},{28,29},{1,0},{5... | collective-permute-start | bytes 589832 | tf_op jit(solution)/shard_map/ppermute | solution.py:32
  65.4 6.3 %collective-permute-start.1 = (bf16[24,4096]{1,0:T(8,128)(2,1)S(1)}, bf16[24,4096]{1,0:T(8,128)(2,1)S(1)}, u32[]{:S(2)}, u32[]{:S(2)}) collective-permute-start(bf16[24,4096]{1,0:T(8,128)(2,1)S(1)} %bitcast.89), channel_id=1, source_target_pairs={{0,16},{4,20},{8,24},{12,28},{16,1},{20,5},{24,9},{28,13},{1,17},{... | collective-permute-start | bytes 589832 | tf_op jit(solution)/shard_map/ppermute | solution.py:32
  65.4 6.2 %collective-permute-start = (bf16[24,4096]{1,0:T(8,128)(2,1)S(1)}, bf16[24,4096]{1,0:T(8,128)(2,1)S(1)}, u32[]{:S(2)}, u32[]{:S(2)}) collective-permute-start(bf16[24,4096]{1,0:T(8,128)(2,1)S(1)} %bitcast.90), channel_id=1, source_target_pairs={{0,17},{4,21},{8,25},{12,29},{16,0},{20,4},{24,8},{28,12},{1,16},{... | collective-permute-start | bytes 589832 | tf_op jit(solution)/shard_map/ppermute | solution.py:32
  71.7 23.7 %collective-permute-start.4 = (bf16[96,4096]{1,0:T(8,128)(2,1)S(1)}, bf16[96,4096]{1,0:T(8,128)(2,1)S(1)}, u32[]{:S(2)}, u32[]{:S(2)}) collective-permute-start(bf16[96,4096]{1,0:T(8,128)(2,1)S(1)} %constant_dynamic-update-slice_fusion.refs_0_), channel_id=1, source_target_pairs={{0,224},{4,228},{8,232},{12,236},{16,240},{20,244},{24,248},{28,25... | collective-permute-start | bytes 2359304 | tf_op jit(solution)/shard_map/ppermute | solution.py:32
  71.8 23.5 %collective-permute-start.3 = (bf16[96,4096]{1,0:T(8,128)(2,1)S(1)}, bf16[96,4096]{1,0:T(8,128)(2,1)S(1)}, u32[]{:S(2)}, u32[]{:S(2)}) collective-permute-start(bf16[96,4096]{1,0:T(8,128)(2,1)S(1)} %constant_dynamic-update-slice_fusion.refs_0_), channel_id=1, source_target_pairs={{0,32},{4,36},{8,40},{12,44},{16,48},{20,52},{24,56},{28,60},{1,33... | collective-permute-start | bytes 2359304 | tf_op jit(solution)/shard_map/ppermute | solution.py:32
  73.3 22.1 %collective-permute-start.8 = (bf16[24,4096]{1,0:T(8,128)(2,1)S(1)}, bf16[24,4096]{1,0:T(8,128)(2,1)S(1)}, u32[]{:S(2)}, u32[]{:S(2)}) collective-permute-start(bf16[24,4096]{1,0:T(8,128)(2,1)S(1)} %collective-permute-done.2), channel_id=1, source_target_pairs={{2,194},{6,198},{10,202},{14,206},{18,210},{22,214},{26,218},{30,2... | collective-permute-start | bytes 589832 | tf_op jit(solution)/shard_map/ppermute | solution.py:32
  78.5 16.8 %collective-permute-start.6 = (bf16[24,4096]{1,0:T(8,128)(2,1)S(1)}, bf16[24,4096]{1,0:T(8,128)(2,1)S(1)}, u32[]{:S(2)}, u32[]{:S(2)}) collective-permute-start(bf16[24,4096]{1,0:T(8,128)(2,1)S(1)} %collective-permute-done.2), channel_id=1, source_target_pairs={{2,226},{6,230},{10,234},{14,238},{18,242},{22,246},{26,250},{30,2... | collective-permute-start | bytes 589832 | tf_op jit(solution)/shard_map/ppermute | solution.py:32
  80.5 14.8 %collective-permute-start.7 = (bf16[24,4096]{1,0:T(8,128)(2,1)S(1)}, bf16[24,4096]{1,0:T(8,128)(2,1)S(1)}, u32[]{:S(2)}, u32[]{:S(2)}) collective-permute-start(bf16[24,4096]{1,0:T(8,128)(2,1)S(1)} %collective-permute-done.5), channel_id=1, source_target_pairs={{2,34},{6,38},{10,42},{14,46},{18,50},{22,54},{26,58},{30,62},{3,3... | collective-permute-start | bytes 589832 | tf_op jit(solution)/shard_map/ppermute | solution.py:32
  83.8 2.0 copy-start.1
  85.9 2.0 copy-start.3
  87.9 2.0 copy-start.4
  95.2 1.2 copy-start.6
  95.4 3.8 %copy-start.2 = (bf16[1,4096,448]{1,2,0:T(8,128)(2,1)S(1)}, bf16[1,4096,448]{1,2,0:T(8,128)(2,1)}, u32[]{:S(2)}) copy-start(bf16[1,4096,448]{1,2,0:T(8,128)(2,1)} %param.15) | copy-start | bytes 11010052
  96.4 12.3 %collective-permute-start.12 = (bf16[96,4096]{1,0:T(8,128)(2,1)S(1)}, bf16[96,4096]{1,0:T(8,128)(2,1)S(1)}, u32[]{:S(2)}, u32[]{:S(2)}) collective-permute-start(bf16[96,4096]{1,0:T(8,128)(2,1)S(1)} %get-tuple-element.65), channel_id=1, source_target_pairs={{0,32},{4,36},{8,40},{12,44},{16,48},{20,52},{24,56},{28,60},{1,33... | collective-permute-start | bytes 2359304 | tf_op jit(solution)/shard_map/ppermute | solution.py:32
  96.4 12.3 %collective-permute-start.9 = (bf16[96,4096]{1,0:T(8,128)(2,1)S(1)}, bf16[96,4096]{1,0:T(8,128)(2,1)S(1)}, u32[]{:S(2)}, u32[]{:S(2)}) collective-permute-start(bf16[96,4096]{1,0:T(8,128)(2,1)S(1)} %get-tuple-element.64), channel_id=1, source_target_pairs={{0,224},{4,228},{8,232},{12,236},{16,240},{20,244},{24,248},{28,25... | collective-permute-start | bytes 2359304 | tf_op jit(solution)/shard_map/ppermute | solution.py:32
  106.3 27.9 %copy-start.8 = (f32[96,4096]{1,0:T(8,128)}, f32[96,4096]{1,0:T(8,128)S(1)}, u32[]{:S(2)}) copy-start(f32[96,4096]{1,0:T(8,128)S(1)} %get-tuple-element.43) | copy-start | bytes 4718596
  108.8 12.3 %collective-permute-start.13 = (bf16[96,4096]{1,0:T(8,128)(2,1)S(1)}, bf16[96,4096]{1,0:T(8,128)(2,1)S(1)}, u32[]{:S(2)}, u32[]{:S(2)}) collective-permute-start(bf16[96,4096]{1,0:T(8,128)(2,1)S(1)} %collective-permute-done.12.refs_1_), channel_id=1, source_target_pairs={{0,32},{4,36},{8,40},{12,44},{16,48},{20,52},{24,56},{28,60},{1,33... | collective-permute-start | bytes 2359304 | tf_op jit(solution)/shard_map/ppermute | solution.py:32
  108.9 13.0 %collective-permute-start.10 = (bf16[96,4096]{1,0:T(8,128)(2,1)S(1)}, bf16[96,4096]{1,0:T(8,128)(2,1)S(1)}, u32[]{:S(2)}, u32[]{:S(2)}) collective-permute-start(bf16[96,4096]{1,0:T(8,128)(2,1)S(1)} %broadcast_select_fusion.1), channel_id=1, source_target_pairs={{0,224},{4,228},{8,232},{12,236},{16,240},{20,244},{24,248},{28,25... | collective-permute-start | bytes 2359304 | tf_op jit(solution)/shard_map/ppermute | solution.py:32
  117.6 4.3 %copy-start.12 = (f32[96,4096]{1,0:T(8,128)}, f32[96,4096]{1,0:T(8,128)S(1)}, u32[]{:S(2)}) copy-start(f32[96,4096]{1,0:T(8,128)S(1)} %get-tuple-element.42) | copy-start | bytes 4718596
  121.2 7.5 %collective-permute-start.14 = (bf16[48,4096]{1,0:T(8,128)(2,1)S(1)}, bf16[48,4096]{1,0:T(8,128)(2,1)S(1)}, u32[]{:S(2)}, u32[]{:S(2)}) collective-permute-start(bf16[48,4096]{1,0:T(8,128)(2,1)S(1)} %slice.52), channel_id=1, source_target_pairs={{0,32},{4,36},{8,40},{12,44},{16,48},{20,52},{24,56},{28,60},{1,33... | collective-permute-start | bytes 1179656 | tf_op jit(solution)/shard_map/ppermute | solution.py:32
  121.9 6.7 %collective-permute-start.11 = (bf16[48,4096]{1,0:T(8,128)(2,1)S(1)}, bf16[48,4096]{1,0:T(8,128)(2,1)S(1)}, u32[]{:S(2)}, u32[]{:S(2)}) collective-permute-start(bf16[48,4096]{1,0:T(8,128)(2,1)S(1)} %slice.64), channel_id=1, source_target_pairs={{0,224},{4,228},{8,232},{12,236},{16,240},{20,244},{24,248},{28,25... | collective-permute-start | bytes 1179656 | tf_op jit(solution)/shard_map/ppermute | solution.py:32
  128.6 18.8 %copy-start.5 = (f32[96,4096]{1,0:T(8,128)}, f32[96,4096]{1,0:T(8,128)S(1)}, u32[]{:S(2)}) copy-start(f32[96,4096]{1,0:T(8,128)S(1)} %get-tuple-element.39) | copy-start | bytes 4718596
  135.3 12.1 %collective-permute-start.15 = (bf16[96,4096]{1,0:T(8,128)(2,1)S(1)}, bf16[96,4096]{1,0:T(8,128)(2,1)S(1)}, u32[]{:S(2)}, u32[]{:S(2)}) collective-permute-start(bf16[96,4096]{1,0:T(8,128)(2,1)S(1)} %get-tuple-element.57), channel_id=1, source_target_pairs={{0,32},{4,36},{8,40},{12,44},{16,48},{20,52},{24,56},{28,60},{1,33... | collective-permute-start | bytes 2359304 | tf_op jit(solution)/shard_map/ppermute | solution.py:32
  148.5 12.4 %collective-permute-start.16 = (bf16[96,4096]{1,0:T(8,128)(2,1)}, bf16[96,4096]{1,0:T(8,128)(2,1)}, u32[]{:S(2)}, u32[]{:S(2)}) collective-permute-start(bf16[96,4096]{1,0:T(8,128)(2,1)} %add_convert_fusion.3), channel_id=1, source_target_pairs={{0,32},{4,36},{8,40},{12,44},{16,48},{20,52},{24,56},{28,60},{1,33... | collective-permute-start | bytes 2359304 | tf_op jit(solution)/shard_map/ppermute | solution.py:32
  151.6 12.2 %copy-start.13 = (f32[96,4096]{1,0:T(8,128)S(1)}, f32[96,4096]{1,0:T(8,128)}, u32[]{:S(2)}) copy-start(f32[96,4096]{1,0:T(8,128)} %copy-done.12) | copy-start | bytes 4718596
  151.6 12.2 %collective-permute-start.17 = (bf16[96,4096]{1,0:T(8,128)(2,1)}, bf16[96,4096]{1,0:T(8,128)(2,1)S(1)}, u32[]{:S(2)}, u32[]{:S(2)}) collective-permute-start(bf16[96,4096]{1,0:T(8,128)(2,1)} %get-tuple-element.58), channel_id=1, source_target_pairs={{0,224},{4,228},{8,232},{12,236},{16,240},{20,244},{24,248},{28,25... | collective-permute-start | bytes 2359304 | tf_op jit(solution)/shard_map/ppermute | solution.py:32
  162.7 12.4 %copy-start.11 = (f32[96,4096]{1,0:T(8,128)S(1)}, f32[96,4096]{1,0:T(8,128)}, u32[]{:S(2)}) copy-start(f32[96,4096]{1,0:T(8,128)} %copy-done.10) | copy-start | bytes 4718596
  162.7 12.4 %collective-permute-start.19 = (bf16[96,4096]{1,0:T(8,128)(2,1)S(1)}, bf16[96,4096]{1,0:T(8,128)(2,1)S(1)}, u32[]{:S(2)}, u32[]{:S(2)}) collective-permute-start(bf16[96,4096]{1,0:T(8,128)(2,1)S(1)} %select_convert_fusion), channel_id=1, source_target_pairs={{0,32},{4,36},{8,40},{12,44},{16,48},{20,52},{24,56},{28,60},{1,33... | collective-permute-start | bytes 2359304 | tf_op jit(solution)/shard_map/ppermute | solution.py:32
  164.1 12.0 %collective-permute-start.18 = (bf16[96,4096]{1,0:T(8,128)(2,1)S(1)}, bf16[96,4096]{1,0:T(8,128)(2,1)S(1)}, u32[]{:S(2)}, u32[]{:S(2)}) collective-permute-start(bf16[96,4096]{1,0:T(8,128)(2,1)S(1)} %add_convert_fusion.2), channel_id=1, source_target_pairs={{0,224},{4,228},{8,232},{12,236},{16,240},{20,244},{24,248},{28,25... | collective-permute-start | bytes 2359304 | tf_op jit(solution)/shard_map/ppermute | solution.py:32
  175.3 17.1 %collective-permute-start.23 = (bf16[96,4096]{1,0:T(8,128)(2,1)S(1)}, bf16[96,4096]{1,0:T(8,128)(2,1)S(1)}, u32[]{:S(2)}, u32[]{:S(2)}) collective-permute-start(bf16[96,4096]{1,0:T(8,128)(2,1)S(1)} %add_convert_fusion.1), channel_id=1, source_target_pairs={{0,32},{4,36},{8,40},{12,44},{16,48},{20,52},{24,56},{28,60},{1,33... | collective-permute-start | bytes 2359304 | tf_op jit(solution)/shard_map/ppermute | solution.py:32
  176.1 10.0 %copy-start.9 = (f32[96,4096]{1,0:T(8,128)S(1)}, f32[96,4096]{1,0:T(8,128)}, u32[]{:S(2)}) copy-start(f32[96,4096]{1,0:T(8,128)} %copy-done.8) | copy-start | bytes 4718596
  177.7 9.3 %collective-permute-start.22 = (bf16[24,4096]{1,0:T(8,128)(2,1)S(1)}, bf16[24,4096]{1,0:T(8,128)(2,1)S(1)}, u32[]{:S(2)}, u32[]{:S(2)}) collective-permute-start(bf16[24,4096]{1,0:T(8,128)(2,1)S(1)} %get-tuple-element.61), channel_id=1, source_target_pairs={{2,226},{6,230},{10,234},{14,238},{18,242},{22,246},{26,250},{30,2... | collective-permute-start | bytes 589832 | tf_op jit(solution)/shard_map/ppermute | solution.py:32
  180.9 11.4 %collective-permute-start.21 = (bf16[24,4096]{1,0:T(8,128)(2,1)S(1)}, bf16[24,4096]{1,0:T(8,128)(2,1)S(1)}, u32[]{:S(2)}, u32[]{:S(2)}) collective-permute-start(bf16[24,4096]{1,0:T(8,128)(2,1)S(1)} %get-tuple-element.62), channel_id=1, source_target_pairs={{2,194},{6,198},{10,202},{14,206},{18,210},{22,214},{26,218},{30,2... | collective-permute-start | bytes 589832 | tf_op jit(solution)/shard_map/ppermute | solution.py:32
  182.9 11.5 %copy-start.7 = (f32[96,4096]{1,0:T(8,128)S(1)}, f32[96,4096]{1,0:T(8,128)}, u32[]{:S(2)}) copy-start(f32[96,4096]{1,0:T(8,128)} %copy-done.6) | copy-start | bytes 4718596
  182.9 9.5 %collective-permute-start.20 = (bf16[24,4096]{1,0:T(8,128)(2,1)S(1)}, bf16[24,4096]{1,0:T(8,128)(2,1)S(1)}, u32[]{:S(2)}, u32[]{:S(2)}) collective-permute-start(bf16[24,4096]{1,0:T(8,128)(2,1)S(1)} %get-tuple-element.63), channel_id=1, source_target_pairs={{2,34},{6,38},{10,42},{14,46},{18,50},{22,54},{26,58},{30,62},{3,3... | collective-permute-start | bytes 589832 | tf_op jit(solution)/shard_map/ppermute | solution.py:32
  186.3 8.1 %collective-permute-start.24 = (bf16[96,4096]{1,0:T(8,128)(2,1)S(1)}, bf16[96,4096]{1,0:T(8,128)(2,1)S(1)}, u32[]{:S(2)}, u32[]{:S(2)}) collective-permute-start(bf16[96,4096]{1,0:T(8,128)(2,1)S(1)} %add_convert_fusion), channel_id=1, source_target_pairs={{0,224},{4,228},{8,232},{12,236},{16,240},{20,244},{24,248},{28,25... | collective-permute-start | bytes 2359304 | tf_op jit(solution)/shard_map/ppermute | solution.py:32
  192.5 9.8 %collective-permute-start.25 = (bf16[24,4096]{1,0:T(8,128)(2,1)S(1)}, bf16[24,4096]{1,0:T(8,128)(2,1)S(1)}, u32[]{:S(2)}, u32[]{:S(2)}) collective-permute-start(bf16[24,4096]{1,0:T(8,128)(2,1)S(1)} %fusion.12), channel_id=1, source_target_pairs={{2,194},{6,198},{10,202},{14,206},{18,210},{22,214},{26,218},{30,2... | collective-permute-start | bytes 589832 | tf_op jit(solution)/shard_map/ppermute | solution.py:32
  194.8 28.9 %copy-start.16 = (bf16[128,256]{1,0:T(8,128)(2,1)S(1)}, bf16[128,256]{1,0:T(8,128)(2,1)}, u32[]{:S(2)}) copy-start(bf16[128,256]{1,0:T(8,128)(2,1)} %param.12) | copy-start | bytes 196612
  194.9 7.7 %collective-permute-start.28 = (bf16[24,4096]{1,0:T(8,128)(2,1)S(1)}, bf16[24,4096]{1,0:T(8,128)(2,1)S(1)}, u32[]{:S(2)}, u32[]{:S(2)}) collective-permute-start(bf16[24,4096]{1,0:T(8,128)(2,1)S(1)} %fusion.10), channel_id=1, source_target_pairs={{0,1},{4,5},{8,9},{12,13},{16,17},{20,21},{24,25},{28,29},{1,0},{5... | collective-permute-start | bytes 589832 | tf_op jit(solution)/shard_map/ppermute | solution.py:32
  197.3 7.3 %collective-permute-start.26 = (bf16[24,4096]{1,0:T(8,128)(2,1)S(1)}, bf16[24,4096]{1,0:T(8,128)(2,1)S(1)}, u32[]{:S(2)}, u32[]{:S(2)}) collective-permute-start(bf16[24,4096]{1,0:T(8,128)(2,1)S(1)} %get-tuple-element.59), channel_id=1, source_target_pairs={{0,16},{4,20},{8,24},{12,28},{16,1},{20,5},{24,9},{28,13},{1,17},{... | collective-permute-start | bytes 589832 | tf_op jit(solution)/shard_map/ppermute | solution.py:32
  197.3 7.3 %collective-permute-start.27 = (bf16[24,4096]{1,0:T(8,128)(2,1)S(1)}, bf16[24,4096]{1,0:T(8,128)(2,1)S(1)}, u32[]{:S(2)}, u32[]{:S(2)}) collective-permute-start(bf16[24,4096]{1,0:T(8,128)(2,1)S(1)} %get-tuple-element.60), channel_id=1, source_target_pairs={{0,17},{4,21},{8,25},{12,29},{16,0},{20,4},{24,8},{28,12},{1,16},{... | collective-permute-start | bytes 589832 | tf_op jit(solution)/shard_map/ppermute | solution.py:32
  (1 other events, 1.2 us)
